TPU v7x, 128 devices: a whole 4x4x4 slice. The times are simulated.
128 devices in a mesh: seq: 8 (over z, core), head: 16 (over y, x).
Axes of the slice: x: 4, y: 4, z: 4, core: 2. Of those that a mesh axis runs over, the one named last changes fastest.
Arguments:
- inputs: bfloat16 [2048, 2304], P('seq', 'head'), may hold values from -6 to 6
- output_grad: bfloat16 [2048, 2304], P('seq', 'head'), may hold values from -6 to 6
- w_query: bfloat16 [2304, 4096], P(None, 'head'), may hold values from -0.1875 to 0.1875
- w_key: bfloat16 [2304, 4096], P(None, 'head'), may hold values from -0.125 to 0.125
- w_value: bfloat16 [2304, 4096], P(None, 'head'), may hold values from -0.125 to 0.125
- w_output: bfloat16 [4096, 2304], P('head'), may hold values from -0.09375 to 0.09375
- gate_log: float32 [2048, 4096], P('seq', 'head'), may hold values from -3 to 0
- beta_gate: float32 [32, 2048], P('head', 'seq'), may hold values from 0.02 to 0.7
- initial_state: float32 [32, 128, 128], P('head'), may hold values from -4 to 4
- doc_starts: int32 [4], replicated, may hold values from 1920 to 2047, as said below
Outputs:
- input_grad: bfloat16 [2048, 2304], P('seq', 'head')
- gate_grad: float32 [2048, 4096], P('seq', 'head')
- beta_grad: float32 [32, 2048], P('head', 'seq')
- state_grad: float32 [32, 128, 128], P('head')
Inputs may be any that keep to these rules, and one draw needn't show every extreme that they name: `doc_starts`: increasing and distinct; each is a position at which a new document begins; the smallest is 1920 and the largest is 2047; the tokens before the smallest continue a document that began before the window, whose state is initial_state.
All inputs are finite; a program needn't handle non-finite values.
Results may differ from a plain program's by a relative error of at most 0.02.
Values may be sent and summed in bfloat16 or wider, within the bound.
A program may use at most 64 MiB of HBM per device.

v0:
```python
import jax
import jax.numpy as jnp
from jax import lax
from jax.sharding import PartitionSpec as P

BLOCK = 64


EPSILON = 1e-06
MAXIMUM_PRECISE = lax.Precision.HIGHEST


def shifted(block, axis, distance):
    devices = range(lax.axis_size(axis))
    route = [(i - distance, i) for i in devices if i - distance in devices]
    return lax.ppermute(block, axis, route)


def unit_rows(raw_rows):
    return raw_rows * lax.rsqrt(jnp.sum(raw_rows * raw_rows, axis=-1, keepdims=True) + EPSILON)


def head_major(matrix, head_count, length):
    tokens_here, columns = matrix.shape
    return matrix.reshape(
        tokens_here // length, length, head_count, columns // head_count
    ).transpose(0, 2, 1, 3)


def block_terms(query_raw, keys_raw, value_rows, gate_logs, beta_rows, segment):
    length = query_raw.shape[2]
    queries = unit_rows(query_raw)
    keys_unit = unit_rows(keys_raw)
    cumulative = jnp.cumsum(gate_logs, axis=2)
    middle = cumulative[:, :, length // 2 - 1 : length // 2, :]
    growth = jnp.exp(cumulative - middle)
    shrunk = keys_unit * jnp.exp(middle - cumulative)
    row_ids = lax.broadcasted_iota(jnp.int32, (length, length), 0)
    col_ids = lax.broadcasted_iota(jnp.int32, (length, length), 1)
    same_doc = segment[:, :, None] == segment[:, None, :]
    strict = jnp.logical_and(same_doc, row_ids > col_ids).astype(jnp.float32)[:, None]
    causal = jnp.logical_and(same_doc, row_ids >= col_ids).astype(jnp.float32)[:, None]
    key_key = (
        jnp.einsum("nhic,nhjc->nhij", keys_unit * growth, shrunk, precision=MAXIMUM_PRECISE)
        * strict
    )
    query_key_scores = (
        jnp.einsum("nhic,nhjc->nhij", queries * growth, shrunk, precision=MAXIMUM_PRECISE) * causal
    )
    system = jnp.eye(length, dtype=jnp.float32) + beta_rows[..., None] * key_key
    opening = (segment == 0).astype(jnp.float32)[:, None, :, None]
    entry_scale = jnp.exp(cumulative) * opening
    right_side = beta_rows[..., None] * jnp.concatenate(
        [value_rows, keys_unit * entry_scale], axis=-1
    )
    solved = lax.linalg.triangular_solve(
        system, right_side, left_side=True, lower=True, unit_diagonal=True
    )
    value_width = value_rows.shape[-1]
    closing = (segment == segment[:, -1:]).astype(jnp.float32)[:, None, :, None]
    outgoing_state = keys_unit * jnp.exp(cumulative[:, :, -1:, :] - cumulative) * closing
    passed_through = (
        jnp.exp(cumulative[:, :, -1, :]) * (segment[:, -1] == 0).astype(jnp.float32)[:, None, None]
    )
    return (
        queries * entry_scale,
        query_key_scores,
        solved[..., :value_width],
        solved[..., value_width:],
        outgoing_state,
        passed_through,
    )


def state_pass(block_parts, start_state, with_output):

    def advance(carried_state, block_item):
        (
            incoming_state,
            query_key_scores,
            baseline_rows,
            coupled_terms,
            outgoing_state,
            passed_through,
        ) = block_item
        blended_rows = baseline_rows - jnp.einsum(
            "zpe,zei->zpi", coupled_terms, carried_state, precision=MAXIMUM_PRECISE
        )
        updated_state = passed_through[..., None] * carried_state + jnp.einsum(
            "fgm,fgo->fmo", outgoing_state, blended_rows, precision=MAXIMUM_PRECISE
        )
        if with_output:
            state_readout = jnp.einsum(
                "zpe,zei->zpi", incoming_state, carried_state, precision=MAXIMUM_PRECISE
            ) + jnp.einsum(
                "abe,aex->abx", query_key_scores, blended_rows, precision=MAXIMUM_PRECISE
            )
            return (updated_state, state_readout)
        return (updated_state, None)

    return lax.scan(advance, start_state, block_parts)


def combine(earlier, later_pair):
    key_width = later_pair.shape[1]
    composed = jnp.einsum(
        "hij,hjk->hik", later_pair[..., :key_width], earlier, precision=MAXIMUM_PRECISE
    )
    return composed + jnp.concatenate(
        [jnp.zeros_like(later_pair[..., :key_width]), later_pair[..., key_width:]], axis=-1
    )


def back_project(grad_rows, weight):
    return lax.dot_general(
        grad_rows.astype(jnp.bfloat16),
        weight,
        (((1,), (1,)), ((), ())),
        preferred_element_type=jnp.float32,
    )


def per_device(
    inputs,
    output_grad,
    w_query,
    w_key,
    w_value,
    w_output,
    gate_log,
    beta_gate,
    initial_state,
    doc_starts,
):
    head_count = initial_state.shape[0]
    key_width = initial_state.shape[1]
    value_width = initial_state.shape[2]
    tokens_here = inputs.shape[0]
    blocks = tokens_here // BLOCK
    portion = lax.all_gather(inputs, "head", axis=1, tiled=True)
    query_part = jnp.dot(portion, w_query, preferred_element_type=jnp.float32)
    keys_part = jnp.dot(portion, w_key, preferred_element_type=jnp.float32)
    value_part = jnp.dot(portion, w_value, preferred_element_type=jnp.float32)
    attn_grad = lax.dot_general(
        lax.all_gather(output_grad, "head", axis=1, tiled=True),
        w_output,
        (((1,), (1,)), ((), ())),
        preferred_element_type=jnp.float32,
    )
    seq_index = lax.axis_index("seq")
    token_positions = seq_index * tokens_here + lax.iota(jnp.int32, tokens_here)
    starting = jnp.any(token_positions[:, None] == doc_starts[None, :], axis=1).astype(jnp.int32)
    segment = jnp.cumsum(starting.reshape(blocks, BLOCK), axis=1, dtype=jnp.int32)

    def make_terms(query_in, keys_in, value_in, gate_in, beta_in):
        return block_terms(
            head_major(query_in, head_count, BLOCK),
            head_major(keys_in, head_count, BLOCK),
            head_major(value_in, head_count, BLOCK),
            head_major(gate_in, head_count, BLOCK),
            beta_in.reshape(head_count, blocks, BLOCK).transpose(1, 0, 2),
            segment,
        )

    block_parts, terms_pull = jax.vjp(
        make_terms, query_part, keys_part, value_part, gate_log, beta_gate
    )
    identity = jnp.broadcast_to(
        jnp.concatenate(
            [
                jnp.eye(key_width, dtype=jnp.float32),
                jnp.zeros((key_width, value_width), jnp.float32),
            ],
            axis=1,
        ),
        (head_count, key_width, key_width + value_width),
    )
    zero_base = jnp.zeros(block_parts[2].shape[:-1] + (key_width,), jnp.float32)
    widened = (
        block_parts[0],
        block_parts[1],
        jnp.concatenate([zero_base, block_parts[2]], axis=-1),
        block_parts[3],
        block_parts[4],
        block_parts[5],
    )
    own_pair, unused = state_pass(widened, identity, False)

    def forward_step(step_index, current):
        composed = shifted(combine(current, own_pair).astype(jnp.bfloat16), "seq", 1).astype(
            jnp.float32
        )
        return jnp.where(seq_index == 0, identity, composed)

    prefix = lax.fori_loop(0, lax.axis_size("seq") - 1, forward_step, identity)
    incoming_state = (
        jnp.einsum(
            "hij,hjk->hik", prefix[..., :key_width], initial_state, precision=MAXIMUM_PRECISE
        )
        + prefix[..., key_width:]
    )

    def run_states(parts_in, state_in):
        return state_pass(parts_in, state_in, True)

    (last_state, state_readout), state_pull = jax.vjp(run_states, block_parts, incoming_state)
    grad_rows = head_major(attn_grad, head_count, BLOCK)
    first_terms, local_back = state_pull((jnp.zeros_like(last_state), grad_rows))
    share = jnp.einsum(
        "hji,hjk->hik", prefix[..., :key_width], local_back, precision=MAXIMUM_PRECISE
    )
    state_grad = lax.psum(share.astype(jnp.bfloat16), "seq").astype(jnp.float32)
    transposed = jnp.swapaxes(own_pair[..., :key_width], 1, 2)

    def backward_step(step_index, current):
        handed = local_back + jnp.einsum(
            "hij,hjk->hik", transposed, current, precision=MAXIMUM_PRECISE
        )
        return shifted(handed.astype(jnp.bfloat16), "seq", -1).astype(handed.dtype)

    state_out_grad = lax.fori_loop(
        0, lax.axis_size("seq") - 1, backward_step, jnp.zeros_like(local_back)
    )
    second_terms, unused_back = state_pull((state_out_grad, jnp.zeros_like(grad_rows)))
    total_terms = jax.tree.map(jnp.add, first_terms, second_terms)
    query_grad, keys_grad, value_grad, gate_grad, beta_grad = terms_pull(total_terms)
    partial_value = (
        back_project(query_grad, w_query)
        + back_project(keys_grad, w_key)
        + back_project(value_grad, w_value)
    )
    input_grad = lax.psum_scatter(
        partial_value.astype(jnp.bfloat16), "head", scatter_dimension=1, tiled=True
    )
    return (input_grad, gate_grad, beta_grad, state_grad)


def solution(mesh):
    return jax.shard_map(
        per_device,
        mesh=mesh,
        in_specs=(
            P("seq", "head"),
            P("seq", "head"),
            P(None, "head"),
            P(None, "head"),
            P(None, "head"),
            P("head", None),
            P("seq", "head"),
            P("head", "seq"),
            P("head", None, None),
            P(),
        ),
        out_specs=(P("seq", "head"), P("seq", "head"), P("head", "seq"), P("head", None, None)),
        check_vma=False,
    )
```

profile of v0, /device:TPU:0, one launch (start us, length us, event | category | flops | bytes accessed | tf_op | source)
XLA Modules:
  0.0 513.5 jit_solution(18237439765985559975)
XLA Ops:
  13.3 42.4 %all-gather.3.cloned.1.call-done = bf16[256,2304]{0,1:T(8,128)(2,1)} async-done(((bf16[256,144]{0,1:T(8,128)(2,1)}), bf16[256,2304]{0,1:T(8,128)(2,1)}) %all-gather.3.cloned.1.call-update) | async-done | bytes 1179664 | tf_op jit(solution)/shard_map/all_gather | solution.py:140
  55.6 2.1 fusion.175
  58.1 1.8 fusion.173
  61.8 40.1 %custom-call.7 = f32[4,2,1,64,64]{3,4,2,1,0:T(8,128)S(1)} custom-call(f32[4,2,1,64,64]{4,3,2,1,0:T(8,128)} %add_bitcast_fusion), custom_call_target="InvertDiagBlocksLowerTriangular" | custom-call | tf_op jit(solution)/shard_map/jvp()/triangular_solve | solution.py:56
  101.8 2.9 fusion.176
  104.8 1.8 reshape.195
  111.1 9.5 %while.103 = (s32[]{:T(128)}, f32[2,128,256]{2,1,0:T(8,128)S(1)}, f32[4,2,128]{2,1,0:T(2,128)}, f32[4,2,64,128]{3,2,1,0:T(8,128)S(1)}, f32[4,2,64,256]{3,2,1,0:T(8,128)}, /*index=5*/f32[4,2,64,128]{3,2,1,0:T(8,128)}, s32[]{:T(128)}) while((s32[]{:T(128)}, f32[2,128,256]{2,1,0:T(8,128)S(1)}, f32[4,2,128]{2,1,0:T(2,128)}, ...), condition=%wide.region_5.6_spmd, body=%wide.region_4.5_spmd.sunk | while | flops 100827136 | bytes 1314901 | solution.py:101
  120.6 1.4 convolution_multiply_fusion
  121.9 1.8 copy.106
  125.5 60.3 %while.106 = (s32[]{:T(128)}, f32[2,128,256]{2,1,0:T(8,128)S(1)}, pred[]{:T(512)}, f32[2,128,256]{2,1,0:T(8,128)S(1)}, f32[128,256]{1,0:T(8,128)}, /*index=5*/s32[]{:T(128)}) while((s32[]{:T(128)}, f32[2,128,256]{2,1,0:T(8,128)S(1)}, pred[]{:T(512)}, f32[2,128,256]{2,1,0:T(8,128)S(1)}, f32[128,256]{1,0:T(8,128)}, ...), condition=%wide.region_7.8_spmd.clone, body=%wide.region_6.7_spmd.clone.sunk | while | flops 100925440 | bytes 2490506 | solution.py:195
  131.7 5.2 %collective-permute-start = (bf16[2,128,256]{2,1,0:T(8,128)(2,1)}, bf16[2,128,256]{2,1,0:T(8,128)(2,1)S(1)}, u32[]{:S(2)}, u32[]{:S(2)}) collective-permute-start(bf16[2,128,256]{2,1,0:T(8,128)(2,1)} %fusion.291), channel_id=1, source_target_pairs={{0,16},{16,32},{32,48},{48,64},{64,80},{80,96},{96,112},{1,17},{17... | collective-permute-start | bytes 393224 | tf_op jit(solution)/shard_map/while/body/eval_jaxpr/ppermute | solution.py:16
  140.9 5.3 %collective-permute-start = (bf16[2,128,256]{2,1,0:T(8,128)(2,1)}, bf16[2,128,256]{2,1,0:T(8,128)(2,1)S(1)}, u32[]{:S(2)}, u32[]{:S(2)}) collective-permute-start(bf16[2,128,256]{2,1,0:T(8,128)(2,1)} %fusion.291), channel_id=1, source_target_pairs={{0,16},{16,32},{32,48},{48,64},{64,80},{80,96},{96,112},{1,17},{17... | collective-permute-start | bytes 393224 | tf_op jit(solution)/shard_map/while/body/eval_jaxpr/ppermute | solution.py:16
  150.1 5.3 %collective-permute-start = (bf16[2,128,256]{2,1,0:T(8,128)(2,1)}, bf16[2,128,256]{2,1,0:T(8,128)(2,1)S(1)}, u32[]{:S(2)}, u32[]{:S(2)}) collective-permute-start(bf16[2,128,256]{2,1,0:T(8,128)(2,1)} %fusion.291), channel_id=1, source_target_pairs={{0,16},{16,32},{32,48},{48,64},{64,80},{80,96},{96,112},{1,17},{17... | collective-permute-start | bytes 393224 | tf_op jit(solution)/shard_map/while/body/eval_jaxpr/ppermute | solution.py:16
  159.2 5.3 %collective-permute-start = (bf16[2,128,256]{2,1,0:T(8,128)(2,1)}, bf16[2,128,256]{2,1,0:T(8,128)(2,1)S(1)}, u32[]{:S(2)}, u32[]{:S(2)}) collective-permute-start(bf16[2,128,256]{2,1,0:T(8,128)(2,1)} %fusion.291), channel_id=1, source_target_pairs={{0,16},{16,32},{32,48},{48,64},{64,80},{80,96},{96,112},{1,17},{17... | collective-permute-start | bytes 393224 | tf_op jit(solution)/shard_map/while/body/eval_jaxpr/ppermute | solution.py:16
  168.4 5.3 %collective-permute-start = (bf16[2,128,256]{2,1,0:T(8,128)(2,1)}, bf16[2,128,256]{2,1,0:T(8,128)(2,1)S(1)}, u32[]{:S(2)}, u32[]{:S(2)}) collective-permute-start(bf16[2,128,256]{2,1,0:T(8,128)(2,1)} %fusion.291), channel_id=1, source_target_pairs={{0,16},{16,32},{32,48},{48,64},{64,80},{80,96},{96,112},{1,17},{17... | collective-permute-start | bytes 393224 | tf_op jit(solution)/shard_map/while/body/eval_jaxpr/ppermute | solution.py:16
  177.6 5.3 %collective-permute-start = (bf16[2,128,256]{2,1,0:T(8,128)(2,1)}, bf16[2,128,256]{2,1,0:T(8,128)(2,1)S(1)}, u32[]{:S(2)}, u32[]{:S(2)}) collective-permute-start(bf16[2,128,256]{2,1,0:T(8,128)(2,1)} %fusion.291), channel_id=1, source_target_pairs={{0,16},{16,32},{32,48},{48,64},{64,80},{80,96},{96,112},{1,17},{17... | collective-permute-start | bytes 393224 | tf_op jit(solution)/shard_map/while/body/eval_jaxpr/ppermute | solution.py:16
  187.7 16.4 %while.104 = (s32[]{:T(128)}, f32[2,128,128]{2,1,0:T(8,128)S(1)}, f32[4,2,128,128]{3,2,1,0:T(8,128)S(1)}, f32[4,2,128,1]{2,1,3,0:T(2,128)}, f32[4,2,64,128]{3,2,...) while((s32[]{:T(128)}, f32[2,128,128]{2,1,0:T(8,128)S(1)}, ...), condition=%wide.region_9.10_spmd, body=%wide.region_8.9_spmd.sunk | while | flops 50413568 | bytes 1055345 | solution.py:101
  187.7 1.7 bitcast_dynamic-update-slice_fusion.8
  191.8 1.7 bitcast_dynamic-update-slice_fusion.8
  195.9 1.7 bitcast_dynamic-update-slice_fusion.8
  200.0 1.7 bitcast_dynamic-update-slice_fusion.8
  204.1 2.1 fusion.174
  212.3 50.8 %while.107 = (s32[]{:T(128)}, f32[2,128,128]{2,1,0:T(8,128)S(1)}, f32[4,2,64,128]{3,2,1,0:T(8,128)}, f32[4,2,64,64]{3,2,1,0:T(8,128)}, f32[4,2,64,128]{3,2,1,0:T...) while((s32[]{:T(128)}, f32[2,128,128]{2,1,0:T(8,128)S(1)}, ...), condition=%wide.region_13.14_spmd.clone, body=%wide.region_11.13_spmd.clone.sunk | while | flops 176504576 | bytes 2637523 | solution.py:101
  212.3 1.7 fusion.307
  214.0 1.7 bitcast_dynamic-update-slice_fusion.11
  217.7 1.8 fusion.311
  223.3 1.7 fusion.309
  225.0 1.7 fusion.307
  226.7 1.7 bitcast_dynamic-update-slice_fusion.11
  230.4 1.8 fusion.311
  236.0 1.7 fusion.309
  237.7 1.7 fusion.307
  239.4 1.7 bitcast_dynamic-update-slice_fusion.11
  243.1 1.8 fusion.311
  248.7 1.7 fusion.309
  250.4 1.7 fusion.307
  252.1 1.7 bitcast_dynamic-update-slice_fusion.11
  255.8 1.8 fusion.311
  261.4 1.7 fusion.309
  264.0 42.3 %while.108 = (s32[]{:T(128)}, f32[2,128,128]{2,1,0:T(8,128)S(1)}, f32[2,128,128]{2,1,0:T(8,128)S(1)}, f32[2,128,128]{2,1,0:T(8,128)S(1)}, s32[]{:T(128)}, /*index=5*/s32[]{:T(128)}) while((s32[]{:T(128)}, f32[2,128,128]{2,1,0:T(8,128)S(1)}, f32[2,128,128]{2,1,0:T(8,128)S(1)}, f32[2,128,128]{2,1,0:T(8,128)S(1)}, s32[]{:T(128)}, ...), condition=%wide.region_15.16_spmd.clone, body=%wide.region_14.15_spmd.clone.sunk | while | flops 50462720 | bytes 917623 | solution.py:221
  264.3 1.3 collective-permute-start.1
  265.6 4.8 collective-permute-done.1
  272.0 4.9 collective-permute-done.1
  278.5 4.3 collective-permute-done.1
  284.3 4.3 collective-permute-done.1
  290.2 4.3 collective-permute-done.1
  296.1 4.3 collective-permute-done.1
  302.0 4.3 collective-permute-done.1
  310.6 38.1 %while.105 = (s32[]{:T(128)}, f32[2,128,128]{2,1,0:T(8,128)S(1)}, f32[4,2,64,128]{3,2,1,0:T(8,128)}, f32[4,2,64,64]{3,2,1,0:T(8,128)}, f32[4,2,64,128]{3,2,1,0:T...) while((s32[]{:T(128)}, f32[2,128,128]{2,1,0:T(8,128)S(1)}, ...), condition=%wide.region_18.19_spmd, body=%wide.region_16.18_spmd.sunk | while | flops 176373504 | bytes 2370753 | solution.py:101
  351.0 2.0 multiply_reduce_fusion
  353.0 1.3 fusion.117
  354.4 2.4 fusion.157
  356.8 1.5 fusion.160
  359.4 2.3 multiply_reduce_fusion.1
  361.8 1.7 convolution_add_fusion.12
  363.5 3.2 fusion.163
  367.5 1.9 fusion.144
  370.3 2.3 convolution_add_fusion.11
  372.6 1.5 fusion.113
  375.6 2.2 pad_add_fusion.3
  377.8 3.2 reduce_window_sum.35
  382.0 49.0 %all-reduce.10.cloned.1.call-done = bf16[2,128,128]{2,1,0:T(8,128)(2,1)} async-done(((bf16[2,128,128]{2,1,0:T(8,128)(2,1)}), bf16[2,128,128]{2,1,0:T(8,128)(2,1)}) %all-reduce.10.cloned.1.call-update) | async-done | bytes 65552 | tf_op jit(solution)/shard_map/psum | solution.py:212
  431.0 1.5 convert_element_type.118
  432.5 74.5 %reduce-scatter.2.cloned.1.call-done = bf16[256,144]{0,1:T(8,128)(2,1)} async-done(((bf16[256,2304]{0,1:T(8,128)(2,1)}), bf16[256,144]{0,1:T(8,128)(2,1)}) %reduce-scatter.2.cloned.1.call-update) | async-done | bytes 73744 | tf_op jit(solution)/shard_map/reduce_scatter | solution.py:232
  (348 shorter events, 152.5 us)
Async XLA Ops:
  7.2 50.9 %copy-start = (bf16[2304,256]{1,0:T(8,128)(2,1)S(1)}, bf16[2304,256]{1,0:T(8,128)(2,1)}, u32[]{:S(2)}) copy-start(bf16[2304,256]{1,0:T(8,128)(2,1)} %param.24) | copy-start | bytes 3538948
  7.2 4.5 copy-start.48
  7.2 48.4 %all-gather.3.cloned.1.call-start = ((), (), s32[]{:S(2)}) async-start(), calls=%async_computation.1 | async-start | bytes 1253376 | tf_op jit(solution)/shard_map/all_gather | solution.py:140
  7.9 196.2 %all-gather.5.cloned.1.call-start = ((), (), s32[]{:S(2)}) async-start(), calls=%async_computation.2 | async-start | bytes 1253376 | tf_op jit(solution)/shard_map/all_gather | solution.py:145
  8.7 422.3 %all-reduce.10.cloned.1.call-start = ((), (), s32[]{:S(2)}) async-start(), calls=%async_computation.4 | async-start | bytes 131072 | tf_op jit(solution)/shard_map/psum | solution.py:212
  10.1 97.4 %copy-start.36 = (f32[4,64]{1,0:T(4,128)}, f32[4,64]{1,0:T(4,128)S(1)}, u32[]{:S(2)}) copy-start(f32[4,64]{1,0:T(4,128)S(1)} %get-tuple-element.1173) | copy-start | bytes 3076
  10.1 97.4 %copy-start.39 = (f32[4,64]{1,0:T(4,128)}, f32[4,64]{1,0:T(4,128)S(1)}, u32[]{:S(2)}) copy-start(f32[4,64]{1,0:T(4,128)S(1)} %get-tuple-element.1172) | copy-start | bytes 3076
  10.1 47.6 %copy-start.49 = (f32[4]{0:T(128)}, f32[4]{0:T(128)S(1)}, u32[]{:S(2)}) copy-start(f32[4]{0:T(128)S(1)} %compare_convert_fusion.1) | copy-start | bytes 52
  10.2 100.8 %copy-start.2 = (f32[128,256]{1,0:T(8,128)}, f32[128,256]{1,0:T(8,128)S(1)}, u32[]{:S(2)}) copy-start(f32[128,256]{1,0:T(8,128)S(1)} %pad_convert_fusion) | copy-start | bytes 393220
  11.6 95.9 %copy-start.28 = (f32[4,2,1,128]{3,2,1,0:T(1,128)}, f32[4,2,1,128]{3,2,1,0:T(1,128)S(1)}, u32[]{:S(2)}) copy-start(f32[4,2,1,128]{3,2,1,0:T(1,128)S(1)} %get-tuple-element.1168) | copy-start | bytes 12292
  11.8 49.1 %copy-start.31 = (pred[64,64]{1,0:T(8,128)(4,1)}, pred[64,64]{1,0:T(8,128)(4,1)S(1)}, u32[]{:S(2)}) copy-start(pred[64,64]{1,0:T(8,128)(4,1)S(1)} %get-tuple-element.1181) | copy-start | bytes 12292
  12.6 47.6 %copy-start.20 = (f32[4,64,64]{2,1,0:T(8,128)}, f32[4,64,64]{2,1,0:T(8,128)S(1)}, u32[]{:S(2)}) copy-start(f32[4,64,64]{2,1,0:T(8,128)S(1)} %get-tuple-element.1171) | copy-start | bytes 196612
  58.1 2.1 copy-start.34
  60.2 44.6 %copy-start.32 = (f32[4,2,64]{2,1,0:T(2,128)}, f32[4,2,64]{2,1,0:T(2,128)S(1)}, u32[]{:S(2)}) copy-start(f32[4,2,64]{2,1,0:T(2,128)S(1)} %fusion.126) | copy-start | bytes 6148
  60.9 43.9 %copy-start.19 = (f32[4,2,64,64]{3,2,1,0:T(8,128)}, f32[4,2,64,64]{3,2,1,0:T(8,128)S(1)}, u32[]{:S(2)}) copy-start(f32[4,2,64,64]{3,2,1,0:T(8,128)S(1)} %convolution_multiply_fusion.1) | copy-start | bytes 393220
  101.8 6.7 %copy-start.15 = (f32[4,2,1,64,64]{3,4,2,1,0:T(8,128)}, f32[4,2,1,64,64]{3,4,2,1,0:T(8,128)S(1)}, u32[]{:S(2)}) copy-start(f32[4,2,1,64,64]{3,4,2,1,0:T(8,128)S(1)} %custom-call.7) | copy-start | bytes 393220
  107.5 1.8 copy-start.13
  108.6 1.6 copy-start.11
  109.3 1.7 copy-start.3
  111.1 9.5 %copy-start.22 = (f32[4,64,64]{2,1,0:T(8,128)S(1)}, f32[4,64,64]{2,1,0:T(8,128)}, u32[]{:S(2)}) copy-start(f32[4,64,64]{2,1,0:T(8,128)} %get-tuple-element.1170) | copy-start | bytes 196612
  126.6 2.5 collective-permute-start
  131.7 6.4 %collective-permute-start = (bf16[2,128,256]{2,1,0:T(8,128)(2,1)}, bf16[2,128,256]{2,1,0:T(8,128)(2,1)S(1)}, u32[]{:S(2)}, u32[]{:S(2)}) collective-permute-start(bf16[2,128,256]{2,1,0:T(8,128)(2,1)} %fusion.291), channel_id=1, source_target_pairs={{0,16},{16,32},{32,48},{48,64},{64,80},{80,96},{96,112},{1,17},{17... | collective-permute-start | bytes 393224 | tf_op jit(solution)/shard_map/while/body/eval_jaxpr/ppermute | solution.py:16
  140.9 6.5 %collective-permute-start = (bf16[2,128,256]{2,1,0:T(8,128)(2,1)}, bf16[2,128,256]{2,1,0:T(8,128)(2,1)S(1)}, u32[]{:S(2)}, u32[]{:S(2)}) collective-permute-start(bf16[2,128,256]{2,1,0:T(8,128)(2,1)} %fusion.291), channel_id=1, source_target_pairs={{0,16},{16,32},{32,48},{48,64},{64,80},{80,96},{96,112},{1,17},{17... | collective-permute-start | bytes 393224 | tf_op jit(solution)/shard_map/while/body/eval_jaxpr/ppermute | solution.py:16
  150.1 6.5 %collective-permute-start = (bf16[2,128,256]{2,1,0:T(8,128)(2,1)}, bf16[2,128,256]{2,1,0:T(8,128)(2,1)S(1)}, u32[]{:S(2)}, u32[]{:S(2)}) collective-permute-start(bf16[2,128,256]{2,1,0:T(8,128)(2,1)} %fusion.291), channel_id=1, source_target_pairs={{0,16},{16,32},{32,48},{48,64},{64,80},{80,96},{96,112},{1,17},{17... | collective-permute-start | bytes 393224 | tf_op jit(solution)/shard_map/while/body/eval_jaxpr/ppermute | solution.py:16
  159.2 6.5 %collective-permute-start = (bf16[2,128,256]{2,1,0:T(8,128)(2,1)}, bf16[2,128,256]{2,1,0:T(8,128)(2,1)S(1)}, u32[]{:S(2)}, u32[]{:S(2)}) collective-permute-start(bf16[2,128,256]{2,1,0:T(8,128)(2,1)} %fusion.291), channel_id=1, source_target_pairs={{0,16},{16,32},{32,48},{48,64},{64,80},{80,96},{96,112},{1,17},{17... | collective-permute-start | bytes 393224 | tf_op jit(solution)/shard_map/while/body/eval_jaxpr/ppermute | solution.py:16
  168.4 6.5 %collective-permute-start = (bf16[2,128,256]{2,1,0:T(8,128)(2,1)}, bf16[2,128,256]{2,1,0:T(8,128)(2,1)S(1)}, u32[]{:S(2)}, u32[]{:S(2)}) collective-permute-start(bf16[2,128,256]{2,1,0:T(8,128)(2,1)} %fusion.291), channel_id=1, source_target_pairs={{0,16},{16,32},{32,48},{48,64},{64,80},{80,96},{96,112},{1,17},{17... | collective-permute-start | bytes 393224 | tf_op jit(solution)/shard_map/while/body/eval_jaxpr/ppermute | solution.py:16
  177.6 6.5 %collective-permute-start = (bf16[2,128,256]{2,1,0:T(8,128)(2,1)}, bf16[2,128,256]{2,1,0:T(8,128)(2,1)S(1)}, u32[]{:S(2)}, u32[]{:S(2)}) collective-permute-start(bf16[2,128,256]{2,1,0:T(8,128)(2,1)} %fusion.291), channel_id=1, source_target_pairs={{0,16},{16,32},{32,48},{48,64},{64,80},{80,96},{96,112},{1,17},{17... | collective-permute-start | bytes 393224 | tf_op jit(solution)/shard_map/while/body/eval_jaxpr/ppermute | solution.py:16
  264.3 6.1 %collective-permute-start.1 = (bf16[2,128,128]{2,1,0:T(8,128)(2,1)S(1)}, bf16[2,128,128]{2,1,0:T(8,128)(2,1)S(1)}, u32[]{:S(2)}, u32[]{:S(2)}) collective-permute-start(bf16[2,128,128]{2,1,0:T(8,128)(2,1)S(1)} %fusion.315), channel_id=1, source_target_pairs={{16,0},{32,16},{48,32},{64,48},{80,64},{96,80},{112,96},{17,1},{33... | collective-permute-start | bytes 196616 | tf_op jit(solution)/shard_map/while/body/eval_jaxpr/ppermute | solution.py:16
  270.7 6.2 %collective-permute-start.1 = (bf16[2,128,128]{2,1,0:T(8,128)(2,1)S(1)}, bf16[2,128,128]{2,1,0:T(8,128)(2,1)S(1)}, u32[]{:S(2)}, u32[]{:S(2)}) collective-permute-start(bf16[2,128,128]{2,1,0:T(8,128)(2,1)S(1)} %fusion.315), channel_id=1, source_target_pairs={{16,0},{32,16},{48,32},{64,48},{80,64},{96,80},{112,96},{17,1},{33... | collective-permute-start | bytes 196616 | tf_op jit(solution)/shard_map/while/body/eval_jaxpr/ppermute | solution.py:16
  277.2 5.6 %collective-permute-start.1 = (bf16[2,128,128]{2,1,0:T(8,128)(2,1)S(1)}, bf16[2,128,128]{2,1,0:T(8,128)(2,1)S(1)}, u32[]{:S(2)}, u32[]{:S(2)}) collective-permute-start(bf16[2,128,128]{2,1,0:T(8,128)(2,1)S(1)} %fusion.315), channel_id=1, source_target_pairs={{16,0},{32,16},{48,32},{64,48},{80,64},{96,80},{112,96},{17,1},{33... | collective-permute-start | bytes 196616 | tf_op jit(solution)/shard_map/while/body/eval_jaxpr/ppermute | solution.py:16
  283.0 5.6 %collective-permute-start.1 = (bf16[2,128,128]{2,1,0:T(8,128)(2,1)S(1)}, bf16[2,128,128]{2,1,0:T(8,128)(2,1)S(1)}, u32[]{:S(2)}, u32[]{:S(2)}) collective-permute-start(bf16[2,128,128]{2,1,0:T(8,128)(2,1)S(1)} %fusion.315), channel_id=1, source_target_pairs={{16,0},{32,16},{48,32},{64,48},{80,64},{96,80},{112,96},{17,1},{33... | collective-permute-start | bytes 196616 | tf_op jit(solution)/shard_map/while/body/eval_jaxpr/ppermute | solution.py:16
  288.9 5.6 %collective-permute-start.1 = (bf16[2,128,128]{2,1,0:T(8,128)(2,1)S(1)}, bf16[2,128,128]{2,1,0:T(8,128)(2,1)S(1)}, u32[]{:S(2)}, u32[]{:S(2)}) collective-permute-start(bf16[2,128,128]{2,1,0:T(8,128)(2,1)S(1)} %fusion.315), channel_id=1, source_target_pairs={{16,0},{32,16},{48,32},{64,48},{80,64},{96,80},{112,96},{17,1},{33... | collective-permute-start | bytes 196616 | tf_op jit(solution)/shard_map/while/body/eval_jaxpr/ppermute | solution.py:16
  294.8 5.6 %collective-permute-start.1 = (bf16[2,128,128]{2,1,0:T(8,128)(2,1)S(1)}, bf16[2,128,128]{2,1,0:T(8,128)(2,1)S(1)}, u32[]{:S(2)}, u32[]{:S(2)}) collective-permute-start(bf16[2,128,128]{2,1,0:T(8,128)(2,1)S(1)} %fusion.315), channel_id=1, source_target_pairs={{16,0},{32,16},{48,32},{64,48},{80,64},{96,80},{112,96},{17,1},{33... | collective-permute-start | bytes 196616 | tf_op jit(solution)/shard_map/while/body/eval_jaxpr/ppermute | solution.py:16
  300.7 5.6 %collective-permute-start.1 = (bf16[2,128,128]{2,1,0:T(8,128)(2,1)S(1)}, bf16[2,128,128]{2,1,0:T(8,128)(2,1)S(1)}, u32[]{:S(2)}, u32[]{:S(2)}) collective-permute-start(bf16[2,128,128]{2,1,0:T(8,128)(2,1)S(1)} %fusion.315), channel_id=1, source_target_pairs={{16,0},{32,16},{48,32},{64,48},{80,64},{96,80},{112,96},{17,1},{33... | collective-permute-start | bytes 196616 | tf_op jit(solution)/shard_map/while/body/eval_jaxpr/ppermute | solution.py:16
  306.3 4.3 copy-start.1
  348.7 2.3 copy-start.12
  348.7 2.3 copy-start.14
  348.7 2.3 copy-start.16
  349.8 3.2 copy-start.4
  351.0 3.4 copy-start.23
  356.8 5.0 copy-start.9
  358.3 5.1 %copy-start.17 = (f32[4,2,64,128]{3,2,1,0:T(8,128)}, f32[4,2,64,128]{3,2,1,0:T(8,128)S(1)}, u32[]{:S(2)}) copy-start(f32[4,2,64,128]{3,2,1,0:T(8,128)S(1)} %fusion.160) | copy-start | bytes 786436
  359.4 2.4 copy-start.21
  359.4 4.1 copy-start.25
  359.4 4.1 copy-start.26
  359.4 4.1 copy-start.29
  359.4 4.1 copy-start.37
  359.4 4.1 copy-start.40
  363.5 3.2 copy-start.35
  363.5 3.5 copy-start.33
  367.5 2.8 copy-start.5
  370.2 136.7 %reduce-scatter.2.cloned.1.call-start = ((), (), s32[]{:S(2)}) async-start(), calls=%async_computation.3 | async-start | bytes 1253376 | tf_op jit(solution)/shard_map/reduce_scatter | solution.py:232
  370.3 2.3 copy-start.6
  370.3 2.3 copy-start.27
  374.1 1.3 copy-start.45
  374.1 1.4 copy-start.30
  374.1 1.4 copy-start.46
  374.2 1.4 copy-start.47
  374.2 1.4 copy-start.50
  374.2 1.4 copy-start.10
  374.2 1.4 copy-start.18
  374.2 1.4 copy-start.24
  374.2 1.4 copy-start.38
  374.2 1.4 copy-start.41
  (11 other events, 8.2 us)
Sparse Core Ops, SparseCore 0:
  10.2 45.4 all-gather.2
  57.8 43.2 all-gather.4
  370.3 60.6 all-reduce.9
  435.0 71.9 reduce-scatter.1
where the time goes:
time: 517 us; the launch traced here: 513 us
  waiting for transfers between devices  207 us (40%)
  matrix products  136 us (26%)
  other arithmetic  62.8 us (12%)
  local copies, waits for them, and re-layouts  50.2 us (10%)
  starting transfers between devices  42.3 us (8%)
  between operations  14.6 us (3%)
    reduce_scatter x1, waiting for transfers between devices, per_device(): lax.psum_scatter(partial_value.astype(jnp.bfloat16), 'head', scatter_dime...  74.5 us
    psum x1, waiting for transfers between devices, per_device(): state_grad = lax.psum(share.astype(jnp.bfloat16), 'seq').astype(jnp.float32)  49 us
    all_gather x1, waiting for transfers between devices, per_device(): portion = lax.all_gather(inputs, 'head', axis=1, tiled=True)  42.4 us
    ppermute x14, starting transfers between devices, shifted(): return lax.ppermute(block, axis, route)  42.1 us
    another operation x5, other arithmetic, block_terms(): lax.linalg.triangular_solve(system, right_side, left_side=True, lower=Tru...  41 us
    ppermute x14, waiting for transfers between devices, shifted(): return lax.ppermute(block, axis, route)  39.3 us
    dot_general x24, matrix products, advance(): jnp.einsum('zpe,zei->zpi', coupled_terms, carried_state, precision=MAXIMU...  29.6 us
    dot_general x24, matrix products, advance(): jnp.einsum('fgm,fgo->fmo', outgoing_state, blended_rows, precision=MAXIMU...  24.8 us
  transfers between devices with their start and end apart: 18, of which 17 were waited for; matrix products, arithmetic and copies ran while one was open for 23% of the time, Pallas kernels for 0%

commit v1 on v0

v1 whole, which is shorter than its diff:
```python
import jax
import jax.numpy as jnp
from jax import lax
from jax.experimental import pallas as pl
from jax.experimental.pallas import tpu as pltpu
from jax.sharding import PartitionSpec as P

F32, BF = jnp.float32, jnp.bfloat16
MESH = pl.DeviceIdType.MESH
CHUNK = 64
CHUNKS = 4
EPSILON = 1e-06


def mm(a, b, ca=1, cb=0):
    return lax.dot_general(
        a.astype(BF), b.astype(BF), (((ca,), (cb,)), ((), ())), preferred_element_type=F32
    )


def cat(parts, axis=0):
    return jnp.concatenate(parts, axis=axis)


def split(x):
    hi = x.astype(BF)
    return hi, (x - hi.astype(F32)).astype(BF)


def rowsum(x):
    return jnp.sum(x, axis=1, keepdims=True)


def per_head(rows):
    return cat([jnp.broadcast_to(r, (CHUNK, 128)) for r in rows])


def iotas():
    i = lax.broadcasted_iota(jnp.int32, (128, 128), 0)
    j = lax.broadcasted_iota(jnp.int32, (128, 128), 1)
    return i, j


HEADS = (slice(0, CHUNK), slice(CHUNK, 2 * CHUNK))


def invert(n, i, j):
    eye = (i == j).astype(F32)
    d = jnp.where((i >> 4) == (j >> 4), n, 0.0)
    d2 = mm(d, d)
    p = mm(eye - d, eye + d2)
    d4 = mm(d2, d2)
    p = mm(p, eye + d4)
    d8 = mm(d4, d4)
    t = mm(p, eye + d8)
    for s in (4, 5):
        off = jnp.where(((i >> (s + 1)) == (j >> (s + 1))) & ((i >> s) != (j >> s)), n, 0.0)
        t = t - mm(t, mm(off, t))
    return t


(QN, KN, RQ, RK, EO, EG, ES, EX, U_, Y0, BETA) = range(11)
(QG, KG, KS, W_, TK, KO, DO, CAUSAL, STRICT) = range(9)


def segments(ds_ref, t0):
    row = t0 + (lax.broadcasted_iota(jnp.int32, (128, 1), 0) & (CHUNK - 1))
    col = t0 + (lax.broadcasted_iota(jnp.int32, (1, 128), 1) & (CHUNK - 1))
    segr, segc = jnp.zeros_like(row), jnp.zeros_like(col)
    for k in range(4):
        start = ds_ref[k]
        here = (start >= t0).astype(jnp.int32)
        segr = segr + (row >= start).astype(jnp.int32) * here
        segc = segc + (col >= start).astype(jnp.int32) * here
    return segr, segc


def first_pass(c, t0, q, k, v, g, beta, dO, ds_ref, sf, sb, chain, passed):
    i, j = iotas()
    segr, segc = segments(ds_ref, t0)
    same = ((i >> 6) == (j >> 6)) & (segr == segc)
    strict, causal = same & (i > j), same & (i >= j)
    tri = (((i >> 6) == (j >> 6)) & (i >= j)).astype(BF)
    rq = lax.rsqrt(rowsum(q * q) + EPSILON)
    rk = lax.rsqrt(rowsum(k * k) + EPSILON)
    qn, kn = q * rq, k * rk
    hi, lo = split(g)
    G = mm(cat([tri, tri], 1), cat([hi, lo]))
    mid = per_head([G[31:32], G[95:96]])
    last = per_head([G[63:64], G[127:128]])
    opening = (segr == 0).astype(F32)
    final = [segr[63:64], segr[127:128]]
    closing = (segr == cat([jnp.broadcast_to(f, (CHUNK, 1)) for f in final])).astype(F32)
    eg, es = jnp.exp(G - mid), jnp.exp(mid - G)
    eo = jnp.exp(G) * opening
    ex = jnp.exp(last - G) * closing
    kg, qg, ks = (kn * eg).astype(BF), (qn * eg).astype(BF), (kn * es).astype(BF)
    kout = kn * ex
    ap = mm(cat([kg, qg]), ks, 1, 1)
    a = jnp.where(strict, ap[:128], 0.0)
    p = jnp.where(causal, ap[128:], 0.0)
    t = invert(beta * a, i, j)
    uw = mm(t, cat([beta * v, beta * (kn * eo)], 1))
    u, w = uw[:, :128], uw[:, 128:]
    qt = qn * eo - mm(p, w)
    pdo = mm(p, dO, 0, 0)
    yt = mm(t, cat([pdo, kout], 1), 0, 0)
    for h, s in enumerate(HEADS):
        end = CHUNK * h + CHUNK - 1
        keep = jnp.exp(G[end : end + 1]) * (final[h] == 0).astype(F32)
        passed[c, h : h + 1, :] = keep
        kw = mm(kout[s], uw[s], 0, 0)
        chain[c, h, 0] = jnp.where(i == j, keep, 0.0) - kw[:, 128:]
        chain[c, h, 1] = kw[:, :128]
        chain[c, h, 2] = mm(qt[s], dO[s], 0, 0)
    wide = lambda z: jnp.broadcast_to(z, (128, 128))
    for slot, value in (
        (QN, qn), (KN, kn), (RQ, wide(rq)), (RK, wide(rk)), (EO, eo), (EG, eg), (ES, es),
        (EX, ex), (U_, u), (Y0, yt[:, :128]), (BETA, wide(beta)),
    ):
        sf[c, slot] = value
    for slot, value in (
        (QG, qg), (KG, kg), (KS, ks), (W_, w), (TK, yt[:, 128:]), (KO, kout), (DO, dO),
        (CAUSAL, causal.astype(F32)), (STRICT, strict.astype(F32)),
    ):
        sb[c, slot] = value.astype(BF)


def second_pass(c, S, D, sf, sb, passed):
    f = lambda slot: sf[c, slot]
    b = lambda slot: sb[c, slot]
    i, j = iotas()
    S, D = [s.astype(BF) for s in S], [d.astype(BF) for d in D]
    w, tk, dO, beta = b(W_), b(TK), b(DO), f(BETA)
    x = f(U_) - cat([mm(w[s], S[h]) for h, s in enumerate(HEADS)])
    y = f(Y0) + cat([mm(tk[s], D[h]) for h, s in enumerate(HEADS)])
    dbeta = rowsum(y * x) / beta[:, :1]
    dv = beta * y
    xb, yb = x.astype(BF), y.astype(BF)
    pa = mm(cat([dO, yb]), xb, 1, 1)
    dp = jnp.where(b(CAUSAL).astype(F32) > 0, pa[:128], 0.0)
    da = jnp.where(b(STRICT).astype(F32) > 0, -beta * pa[128:], 0.0)
    ys = [mm(cat([dO[s], yb[s]]), S[h], 1, 1) for h, s in enumerate(HEADS)]
    eo = f(EO)
    qs = cat([ys[0][:CHUNK], ys[1][:CHUNK]]) * eo
    ke = cat([ys[0][CHUNK:], ys[1][CHUNK:]]) * (-beta * eo)
    dko = cat([mm(xb[s], D[h], 1, 1) for h, s in enumerate(HEADS)])
    pab = cat([dp, da]).astype(BF)
    qg, kg, ks = b(QG), b(KG), b(KS)
    dqk = mm(pab, ks)
    dqg, dkg = dqk[:128], dqk[128:]
    dks = mm(pab, cat([qg, kg]), 0, 0)
    qn, kn, eg = f(QN), f(KN), f(EG)
    dq = qs + dqg * eg
    dk = ke + dkg * eg + dks * f(ES) + dko * f(EX)
    kd = b(KO).astype(F32) * dko
    dG = (
        qn * qs + qg.astype(F32) * dqg + kg.astype(F32) * dkg
        - ks.astype(F32) * dks + kn * ke - kd
    )
    ends = []
    for h, s in enumerate(HEADS):
        hi, lo = split(S[h].astype(F32) * D[h].astype(F32))
        through = mm(jnp.ones((8, 256), BF), cat([hi, lo], 1), 1, 1)[0:1]
        ends.append(jnp.sum(kd[s], axis=0, keepdims=True) + passed[c, h : h + 1, :] * through)
    hi, lo = split(dG)
    upper = (((i >> 6) == (j >> 6)) & (i <= j)).astype(BF)
    dg = mm(cat([upper, upper], 1), cat([hi, lo])) + per_head(ends)
    dqr = f(RQ) * (dq - qn * rowsum(qn * dq))
    dkr = f(RK) * (dk - kn * rowsum(kn * dk))
    return dqr, dkr, dv, dg, dbeta


def flipped(x):
    x = x.astype(F32)
    tail = cat([x[:, 128:], jnp.zeros((256, 112), F32)], 1)
    return cat([x[:, :128].T, tail.T[:16]]).astype(BF)


def kernel(
    x_ref, og_ref, wq_ref, wk_ref, wv_ref, wo_ref, gate_ref, beta_ref, init_ref, ds_ref,
    ig_ref, gg_ref, bg_ref, sg_ref,
    wcat, wo, wot, xg, raw, gcat, sf, sb, chain, passed, prefix, suffix,
    own, heard, comm, bounds, part, r1, t2, t2f, r2,
    wsem, gsend, grecv, esend, erecv, rsend, rrecv,
):
    seq, head = lax.axis_index("seq"), lax.axis_index("head")
    y, x = head // 4, head % 4
    z, core = seq // 2, seq % 2
    xs = [{"head": y * 4 + (x + o) % 4} for o in (1, 2, 3)]
    ys = [{"head": ((y + o) % 4) * 4 + x} for o in (1, 2, 3)]
    zs = [{"seq": ((z + o) % 4) * 2 + core} for o in (1, 2, 3)]
    sibling = {"seq": z * 2 + (1 - core)}

    loads = [
        pltpu.make_async_copy(ref, wcat.at[:, 256 * n : 256 * n + 256], wsem.at[n])
        for n, ref in enumerate((wq_ref, wk_ref, wv_ref))
    ]
    loads.append(pltpu.make_async_copy(wo_ref, wo, wsem.at[3]))
    for load in loads:
        load.start()

    barrier = pltpu.get_barrier_semaphore()
    partners = xs + ys + zs + [sibling]
    for device in partners:
        pl.semaphore_signal(barrier, inc=1, device_id=device, device_id_type=MESH)

    for item, ref in enumerate((x_ref, og_ref)):
        turned = flipped(ref[...])
        xg[item, 0, y, x] = turned[:, :128]
        xg[item, 1, y, x] = turned[:, 128:]
    pl.semaphore_wait(barrier, len(partners))

    def remote(src, dst, ssem, rsem, device):
        return pltpu.make_async_remote_copy(
            src_ref=src, dst_ref=dst, send_sem=ssem, recv_sem=rsem,
            device_id=device, device_id_type=MESH,
        )

    def gather(item, half, phase):
        axis = xs if (half + phase) % 2 == 0 else ys
        if phase == 0:
            block = xg.at[item, half, y, x]
        else:
            block = xg.at[item, 0, y] if half == 0 else xg.at[item, 1, :, x]
        return [
            remote(block, block, gsend.at[item, half, phase, o], grecv.at[item, half, phase, o],
                   axis[o])
            for o in (1, 0, 2)
        ]

    near = [[gather(item, half, 0) for half in (0, 1)] for item in (0, 1)]
    far = [[gather(item, half, 1) for half in (0, 1)] for item in (0, 1)]
    for item in (0, 1):
        for o in range(3):
            for half in (0, 1):
                near[item][half][o].start()
    for item in (0, 1):
        for half in (0, 1):
            for copy in near[item][half]:
                copy.wait_recv()
            for copy in far[item][half]:
                copy.start()

    loads[3].wait()
    for n in range(18):
        wot[128 * n : 128 * n + 128, :] = wo[:, 128 * n : 128 * n + 128].T
    for load in loads[:3]:
        load.wait()

    def project(item, weight, columns):
        for half in (0, 1):
            for copy in far[item][half]:
                copy.wait_recv()
            rows = xg[item, half].reshape(2304, 128)
            raw[128 * half : 128 * half + 128, columns] = mm(rows, weight[...], 0, 0)

    project(0, wcat, slice(0, 768))
    project(1, wot, slice(768, 1024))

    def stacked(ref, c, first):
        t = slice(CHUNK * c, CHUNK * c + CHUNK)
        return cat([ref[t, first : first + 128], ref[t, first + 128 : first + 256]])

    diagonal = (
        lax.broadcasted_iota(jnp.int32, (CHUNK, CHUNK), 0)
        == lax.broadcasted_iota(jnp.int32, (CHUNK, CHUNK), 1)
    )
    for c in range(CHUNKS):
        t = slice(CHUNK * c, CHUNK * c + CHUNK)
        beta = cat([rowsum(jnp.where(diagonal, beta_ref[h : h + 1, t], 0.0)) for h in (0, 1)])
        first_pass(
            c, seq * 256 + CHUNK * c,
            stacked(raw, c, 0), stacked(raw, c, 256), stacked(raw, c, 512),
            stacked(gate_ref, c, 0), beta, stacked(raw, c, 768),
            ds_ref, sf, sb, chain, passed,
        )

    for h in (0, 1):
        m, v = chain[0, h, 0], chain[0, h, 1]
        prefix[h, 0, :, :128], prefix[h, 0, :, 128:] = m, v
        for n in (1, 2, 3):
            step = mm(chain[n, h, 0], cat([m, v], 1))
            m, v = step[:, :128], step[:, 128:] + chain[n, h, 1]
            if n < 3:
                prefix[h, n, :, :128], prefix[h, n, :, 128:] = m, v
        l = chain[3, h, 2]
        suffix[h, 2, :, 128:] = l
        for n in (2, 1, 0):
            l = mm(chain[n, h, 0], l, 0, 0) + chain[n, h, 2]
            if n > 0:
                suffix[h, n - 1, :, 128:] = l
        own[h, 0], own[h, 1], own[h, 2] = m.astype(BF), v.astype(BF), l.astype(BF)

    swap = remote(own.at[1 - core], heard, esend.at[0], erecv.at[0], sibling)
    swap.start()
    for h in (0, 1):
        m = chain[3, h, 0].T
        suffix[h, 2, :, :128] = m
        for n in (2, 1):
            m = mm(chain[n, h, 0], m, 0, 0)
            suffix[h, n - 1, :, :128] = m
    swap.wait_recv()

    first = core == 0
    mine = [own[core, n] for n in range(3)]
    other = [heard[n] for n in range(3)]
    m0, b0, l0 = [jnp.where(first, a, b) for a, b in zip(mine, other)]
    m1, b1, l1 = [jnp.where(first, b, a) for a, b in zip(mine, other)]
    both = mm(m1, cat([m0, b0], 1))
    comm[z, 0] = both[:, :128].astype(BF)
    comm[z, 1] = (both[:, 128:] + b1.astype(F32)).astype(BF)
    comm[z, 2] = (l0.astype(F32) + mm(m0, l1, 0, 0)).astype(BF)
    spread = [
        remote(comm.at[z], comm.at[z], esend.at[1 + o], erecv.at[1 + o], zs[o]) for o in (1, 0, 2)
    ]
    for copy in spread:
        copy.start()
    for copy in spread:
        copy.wait_recv()
    state, entering = init_ref[core], init_ref[core]
    for n in range(3):
        state = mm(comm[n, 0], state) + comm[n, 1].astype(F32)
        entering = jnp.where(z == n + 1, state, entering)
    grad = comm[3, 2].astype(F32)
    leaving = jnp.where(z == 2, grad, 0.0)
    for n in (2, 1, 0):
        grad = mm(comm[n, 0], grad, 0, 0) + comm[n, 2].astype(F32)
        leaving = jnp.where(z == n - 1, grad, leaving)
    after = mm(m0, entering) + b0.astype(F32)
    before = mm(m1, leaving, 0, 0) + l1.astype(F32)
    my_state, sib_state = jnp.where(first, entering, after), jnp.where(first, after, entering)
    my_grad, sib_grad = jnp.where(first, before, leaving), jnp.where(first, leaving, before)
    for n, value in enumerate((sib_state, sib_grad, grad)):
        heard2 = bounds
        heard2[2 + core, n] = value.astype(BF)
    give = remote(bounds.at[2 + core], bounds.at[core], esend.at[4], erecv.at[4], sibling)
    give.start()
    bounds[core, 0], bounds[core, 1] = my_state.astype(BF), my_grad.astype(BF)
    bounds[core, 2] = grad.astype(BF)
    give.wait_recv()

    for h in (0, 1):
        sg_ref[h] = bounds[h, 2].astype(F32)
    S, D = [], []
    for h in (0, 1):
        s, d = bounds[h, 0], bounds[h, 1]
        S.append([s] + [mm(prefix[h, n, :, :128], s) + prefix[h, n, :, 128:] for n in range(3)])
        D.append([mm(suffix[h, n, :, :128], d) + suffix[h, n, :, 128:] for n in range(3)] + [d])
    for c in range(CHUNKS):
        t = slice(CHUNK * c, CHUNK * c + CHUNK)
        dq, dk, dv, dg, dbeta = second_pass(
            c, [S[0][c], S[1][c]], [D[0][c], D[1][c]], sf, sb, passed
        )
        for h, s in enumerate(HEADS):
            for n, value in enumerate((dq, dk, dv)):
                gcat[t, 256 * n + 128 * h : 256 * n + 128 * h + 128] = value[s].astype(BF)
            gg_ref[t, 128 * h : 128 * h + 128] = dg[s]
            bg_ref[h : h + 1, t] = jnp.sum(
                jnp.where(diagonal, dbeta[s], 0.0), axis=0, keepdims=True
            )

    def share(half, target):
        rows = gcat[128 * half : 128 * half + 128, :]
        if half == 0:
            return mm(wcat[pl.ds(pl.multiple_of(576 * target, 16), 576), :], rows, 1, 1)
        return cat([
            mm(wcat[pl.ds(pl.multiple_of(576 * n + 144 * target, 16), 144), :], rows, 1, 1)
            for n in range(4)
        ])

    sums = [[], []]
    for o in (1, 0, 2):
        for half, place, axis in ((0, y, ys), (1, x, xs)):
            part[half, o] = share(half, (place + o + 1) % 4).astype(BF)
            copy = remote(
                part.at[half, o], r1.at[half, o], rsend.at[half, 0, o], rrecv.at[half, 0, o],
                axis[o],
            )
            copy.start()
            sums[half].append(copy)
    ends = [[], []]
    totals = [share(0, y), share(1, x)]
    for half, place, axis in ((0, x, xs), (1, y, ys)):
        total = totals[half]
        for copy in sums[half]:
            copy.wait_recv()
        for o in range(3):
            total = total + r1[half, o].astype(F32)
        t2f[half] = total.reshape(4, 144, 128)
        t2[half] = total.astype(BF).reshape(4, 144, 128)
        for o in (1, 0, 2):
            copy = remote(
                t2.at[half, (place + o + 1) % 4], r2.at[half, o],
                rsend.at[half, 1, o], rrecv.at[half, 1, o], axis[o],
            )
            copy.start()
            ends[half].append(copy)
    done = []
    for half, place in ((0, x), (1, y)):
        total = t2f[half, place]
        for copy in ends[half]:
            copy.wait_recv()
        for o in range(3):
            total = total + r2[half, o].astype(F32)
        done.append(total)
    total = cat(done, 1)
    ig_ref[:, :128] = total[:128].T.astype(BF)
    tail = cat([total[128:], jnp.zeros((112, 256), F32)]).T
    ig_ref[:, 128:] = tail[:, :16].astype(BF)

    for group in near + far:
        for copies in group:
            for copy in copies:
                copy.wait_send()
    for copy in [swap, give] + spread + sums[0] + sums[1] + ends[0] + ends[1]:
        copy.wait_send()


def per_device(*arrays):
    vmem = pl.BlockSpec(memory_space=pltpu.VMEM)
    anywhere = pl.BlockSpec(memory_space=pl.ANY)
    scratch = lambda *shape, dtype=F32: pltpu.VMEM(shape, dtype)
    dma = lambda *shape: pltpu.SemaphoreType.DMA(shape)
    return pl.pallas_call(
        kernel,
        out_shape=(
            jax.ShapeDtypeStruct((256, 144), BF),
            jax.ShapeDtypeStruct((256, 256), F32),
            jax.ShapeDtypeStruct((2, 256), F32),
            jax.ShapeDtypeStruct((2, 128, 128), F32),
        ),
        in_specs=[vmem, vmem] + [anywhere] * 4 + [vmem] * 3
        + [pl.BlockSpec(memory_space=pltpu.SMEM)],
        out_specs=(vmem,) * 4,
        scratch_shapes=[
            scratch(2304, 768, dtype=BF),
            scratch(256, 2304, dtype=BF),
            scratch(2304, 256, dtype=BF),
            scratch(2, 2, 4, 4, 144, 128, dtype=BF),
            scratch(256, 1024),
            scratch(256, 768, dtype=BF),
            scratch(CHUNKS, 11, 128, 128),
            scratch(CHUNKS, 9, 128, 128, dtype=BF),
            scratch(CHUNKS, 2, 3, 128, 128),
            scratch(CHUNKS, 8, 128),
            scratch(2, 3, 128, 256),
            scratch(2, 3, 128, 256),
            scratch(2, 3, 128, 128, dtype=BF),
            scratch(3, 128, 128, dtype=BF),
            scratch(4, 3, 128, 128, dtype=BF),
            scratch(4, 3, 128, 128, dtype=BF),
            scratch(2, 3, 576, 128, dtype=BF),
            scratch(2, 3, 576, 128, dtype=BF),
            scratch(2, 4, 144, 128, dtype=BF),
            scratch(2, 4, 144, 128),
            scratch(2, 3, 144, 128, dtype=BF),
            dma(4), dma(2, 2, 2, 3), dma(2, 2, 2, 3), dma(5), dma(5), dma(2, 2, 3), dma(2, 2, 3),
        ],
        compiler_params=pltpu.CompilerParams(
            collective_id=0, has_side_effects=True, vmem_limit_bytes=48 * 1024 * 1024
        ),
        cost_estimate=pl.CostEstimate(
            flops=3 * 10**9, bytes_accessed=6 * 10**6, transcendentals=3 * 10**5
        ),
    )(*arrays)


def solution(mesh):
    return jax.shard_map(
        per_device,
        mesh=mesh,
        in_specs=(
            P("seq", "head"),
            P("seq", "head"),
            P(None, "head"),
            P(None, "head"),
            P(None, "head"),
            P("head", None),
            P("seq", "head"),
            P("head", "seq"),
            P("head", None, None),
            P(),
        ),
        out_specs=(P("seq", "head"), P("seq", "head"), P("head", "seq"), P("head", None, None)),
        check_vma=False,
    )
```

time: 517 us -> 76 us (0.15)
  waiting for transfers between devices: 207 us -> 0 us
  matrix products: 136 us -> 0 us
  other arithmetic: 62.8 us -> 0 us
  Pallas kernels: 0 us -> 61.7 us
  starting transfers between devices: 42.3 us -> 0 us
  local copies, waits for them, and re-layouts: 50.2 us -> 12.9 us
  between operations: 14.6 us -> 0.67 us
    dot_general x110 -> x0, matrix products: 131 us -> none  [the longest x24 29.6 us: advance(): jnp.einsum('zpe,zei->zpi', coupled_terms, carried_state, precision=MAXIMU...]
    reduce_scatter x1 -> x0, waiting for transfers between devices: 74.5 us -> none  [per_device(): lax.psum_scatter(partial_value.astype(jnp.bfloat16), 'head', scatter_dime...]
    pallas_call x0 -> x1, Pallas kernels: none -> 61.7 us  [per_device(): pl.pallas_call(kernel, out_shape=(jax.ShapeDtypeStruct((256, 144), BF), j...]
    psum x1 -> x0, waiting for transfers between devices: 49 us -> none  [per_device(): state_grad = lax.psum(share.astype(jnp.bfloat16), 'seq').astype(jnp.float32)]
    another operation x8 -> x0, other arithmetic: 44.7 us -> none  [the longest x5 41 us: block_terms(): lax.linalg.triangular_solve(system, right_side, left_side=True, lower=Tru...]
    all_gather x2 -> x0, waiting for transfers between devices: 42.4 us -> none  [the longest x1 42.4 us: per_device(): portion = lax.all_gather(inputs, 'head', axis=1, tiled=True)]
    ppermute x14 -> x0, starting transfers between devices: 42.1 us -> none  [shifted(): return lax.ppermute(block, axis, route)]
    ppermute x14 -> x0, waiting for transfers between devices: 39.3 us -> none  [shifted(): return lax.ppermute(block, axis, route)]
  transfers between devices with their start and end apart: 18 -> 0, of which waited for: 17 -> 0; matrix products, arithmetic and copies ran while one was open for 23% -> 0% of each run, Pallas kernels for 0% -> 0%
where the time goes in v1:
time: 76 us; the launch traced here: 75.3 us
  Pallas kernels  61.7 us (81%)
  local copies, waits for them, and re-layouts  12.9 us (17%)
    pallas_call x1, Pallas kernels, per_device(): pl.pallas_call(kernel, out_shape=(jax.ShapeDtypeStruct((256, 144), BF), j...  61.7 us
    unnamed x21, local copies, waits for them, and re-layouts  12.2 us

profile of v1, /device:TPU:0, one launch (start us, length us, event | category | flops | bytes accessed | tf_op | source)
XLA Modules:
  0.0 75.3 jit_solution(2472737993173764113)
XLA Ops:
  0.6 1.0 %copy.14.x_ref = bf16[256,144]{1,0:T(8,128)(2,1)S(1)} copy(bf16[256,144]{0,1:T(8,128)(2,1)} %param.10) | data formatting | bytes 147456 | tf_op args[0]
  1.6 1.0 %copy.15.og_ref = bf16[256,144]{1,0:T(8,128)(2,1)S(1)} copy(bf16[256,144]{0,1:T(8,128)(2,1)} %param.11) | data formatting | bytes 147456 | tf_op args[1]
  2.6 0.0 copy-start
  2.6 1.3 %copy-done = bf16[2304,256]{1,0:T(8,128)(2,1)S(1)} copy-done((bf16[2304,256]{1,0:T(8,128)(2,1)S(1)}, bf16[2304,256]{1,0:T(8,128)(2,1)}, u32[]{:S(2)}) %copy-start) | copy-done | bytes 1179672
  3.9 0.0 copy-start.1
  3.9 1.3 %copy-done.1 = bf16[2304,256]{1,0:T(8,128)(2,1)S(1)} copy-done((bf16[2304,256]{1,0:T(8,128)(2,1)S(1)}, bf16[2304,256]{1,0:T(8,128)(2,1)}, u32[]{:S(2)}) %copy-start.1) | copy-done | bytes 1179672
  5.2 0.0 copy-start.2
  5.2 1.3 %copy-done.2 = bf16[2304,256]{1,0:T(8,128)(2,1)S(1)} copy-done((bf16[2304,256]{1,0:T(8,128)(2,1)S(1)}, bf16[2304,256]{1,0:T(8,128)(2,1)}, u32[]{:S(2)}) %copy-start.2) | copy-done | bytes 1179672
  6.4 0.0 copy-start.3
  6.4 1.3 %copy-done.3 = bf16[256,2304]{1,0:T(8,128)(2,1)S(1)} copy-done((bf16[256,2304]{1,0:T(8,128)(2,1)S(1)}, bf16[256,2304]{1,0:T(8,128)(2,1)}, u32[]{:S(2)}) %copy-start.3) | copy-done | bytes 1179672
  7.7 0.0 copy-start.4
  7.7 0.9 %copy-done.4 = f32[256,256]{1,0:T(8,128)S(1)} copy-done((f32[256,256]{1,0:T(8,128)S(1)}, f32[256,256]{1,0:T(8,128)}, u32[]{:S(2)}) %copy-start.4) | copy-done | bytes 262168
  8.6 0.0 copy-start.5
  8.7 0.9 %copy-done.5 = f32[2,128,128]{2,1,0:T(8,128)S(1)} copy-done((f32[2,128,128]{2,1,0:T(8,128)S(1)}, f32[2,128,128]{2,1,0:T(8,128)}, u32[]{:S(2)}) %copy-start.5) | copy-done | bytes 131096
  9.6 0.0 copy-start.6
  9.6 0.7 copy-done.6
  10.2 0.0 copy-start.7
  10.2 0.7 copy-done.7
  10.9 61.7 %shard_map.129 = (bf16[256,144]{1,0:T(8,128)(2,1)S(1)}, f32[256,256]{1,0:T(8,128)S(1)}, f32[2,256]{1,0:T(2,128)S(1)}, f32[2,128,128]{2,1,0:T(8,128)S(1)}) custom-call(bf16[256,144]{1,0:T(8,128)(2,1)S(1)} %copy.14.x_ref, bf16[256,144]{1,0:T(8,128)(2,1)S(1)} %copy.15.og_ref, bf16[2304,256]{1,0:T(8,128)(2,1)S(1)} %copy-done, bf16[2304,256]{1,0:T(8,128)(2,1)S(1)} %copy-done.1, ...), custom_call_target="tpu_custom_call" | custom-call | flops 3000000000 | bytes 6000000 | tf_op jit(solution)/shard_map/pallas_call | solution.py:425
  72.6 0.7 copy.16
  73.3 0.7 copy.20
  74.0 0.6 copy.21
  74.6 0.7 copy.22
Async XLA Ops:
  2.6 1.3 %copy-start = (bf16[2304,256]{1,0:T(8,128)(2,1)S(1)}, bf16[2304,256]{1,0:T(8,128)(2,1)}, u32[]{:S(2)}) copy-start(bf16[2304,256]{1,0:T(8,128)(2,1)} %wq_ref.1) | copy-start | bytes 3538948
  3.9 1.3 %copy-start.1 = (bf16[2304,256]{1,0:T(8,128)(2,1)S(1)}, bf16[2304,256]{1,0:T(8,128)(2,1)}, u32[]{:S(2)}) copy-start(bf16[2304,256]{1,0:T(8,128)(2,1)} %wk_ref.1) | copy-start | bytes 3538948
  5.2 1.3 %copy-start.2 = (bf16[2304,256]{1,0:T(8,128)(2,1)S(1)}, bf16[2304,256]{1,0:T(8,128)(2,1)}, u32[]{:S(2)}) copy-start(bf16[2304,256]{1,0:T(8,128)(2,1)} %wv_ref.1) | copy-start | bytes 3538948
  6.4 1.3 %copy-start.3 = (bf16[256,2304]{1,0:T(8,128)(2,1)S(1)}, bf16[256,2304]{1,0:T(8,128)(2,1)}, u32[]{:S(2)}) copy-start(bf16[256,2304]{1,0:T(8,128)(2,1)} %wo_ref.1) | copy-start | bytes 3538948
  7.7 0.9 %copy-start.4 = (f32[256,256]{1,0:T(8,128)S(1)}, f32[256,256]{1,0:T(8,128)}, u32[]{:S(2)}) copy-start(f32[256,256]{1,0:T(8,128)} %gate_ref.1) | copy-start | bytes 786436
  8.6 0.9 %copy-start.5 = (f32[2,128,128]{2,1,0:T(8,128)S(1)}, f32[2,128,128]{2,1,0:T(8,128)}, u32[]{:S(2)}) copy-start(f32[2,128,128]{2,1,0:T(8,128)} %init_ref.1) | copy-start | bytes 393220
  9.6 0.7 copy-start.6
  10.2 0.7 copy-start.7

commit v2 on v1

v2 whole, which is shorter than its diff:
```python
import jax
import jax.numpy as jnp
from jax import lax
from jax.experimental import pallas as pl
from jax.experimental.pallas import tpu as pltpu
from jax.sharding import PartitionSpec as P

F32, BF = jnp.float32, jnp.bfloat16
MESH = pl.DeviceIdType.MESH
CHUNK = 64
CHUNKS = 4
EPSILON = 1e-06


def mm(a, b, ca=1, cb=0):
    return lax.dot_general(
        a.astype(BF), b.astype(BF), (((ca,), (cb,)), ((), ())), preferred_element_type=F32
    )


def cat(parts, axis=0):
    return jnp.concatenate(parts, axis=axis)


def split(x):
    hi = x.astype(BF)
    return hi, (x - hi.astype(F32)).astype(BF)


def rowsum(x):
    return jnp.sum(x, axis=1, keepdims=True)


def per_head(rows):
    return cat([jnp.broadcast_to(r, (CHUNK, 128)) for r in rows])


def iotas():
    i = lax.broadcasted_iota(jnp.int32, (128, 128), 0)
    j = lax.broadcasted_iota(jnp.int32, (128, 128), 1)
    return i, j


HEADS = (slice(0, CHUNK), slice(CHUNK, 2 * CHUNK))


def invert(n, i, j):
    eye = (i == j).astype(F32)
    d = jnp.where((i >> 4) == (j >> 4), n, 0.0)
    d2 = mm(d, d)
    p = mm(eye - d, eye + d2)
    d4 = mm(d2, d2)
    p = mm(p, eye + d4)
    d8 = mm(d4, d4)
    t = mm(p, eye + d8)
    for s in (4, 5):
        off = jnp.where(((i >> (s + 1)) == (j >> (s + 1))) & ((i >> s) != (j >> s)), n, 0.0)
        t = t - mm(t, mm(off, t))
    return t


(QN, KN, RQ, RK, EO, EG, ES, EX, U_, BETA) = range(10)
(QG, KG, KS, W_, TK, KO, PT, CAUSAL, STRICT) = range(9)


def segments(ds_ref, t0):
    row = t0 + (lax.broadcasted_iota(jnp.int32, (128, 1), 0) & (CHUNK - 1))
    col = t0 + (lax.broadcasted_iota(jnp.int32, (1, 128), 1) & (CHUNK - 1))
    segr, segc = jnp.zeros_like(row), jnp.zeros_like(col)
    for k in range(4):
        start = ds_ref[k]
        here = (start >= t0).astype(jnp.int32)
        segr = segr + (row >= start).astype(jnp.int32) * here
        segc = segc + (col >= start).astype(jnp.int32) * here
    return segr, segc


def first_pass(c, t0, q, k, v, g, beta, ds_ref, sf, sb, chain, passed):
    i, j = iotas()
    segr, segc = segments(ds_ref, t0)
    same = ((i >> 6) == (j >> 6)) & (segr == segc)
    strict, causal = same & (i > j), same & (i >= j)
    tri = (((i >> 6) == (j >> 6)) & (i >= j)).astype(BF)
    rq = lax.rsqrt(rowsum(q * q) + EPSILON)
    rk = lax.rsqrt(rowsum(k * k) + EPSILON)
    qn, kn = q * rq, k * rk
    hi, lo = split(g)
    G = mm(cat([tri, tri], 1), cat([hi, lo]))
    mid = per_head([G[31:32], G[95:96]])
    last = per_head([G[63:64], G[127:128]])
    opening = (segr == 0).astype(F32)
    final = [segr[63:64], segr[127:128]]
    closing = (segr == cat([jnp.broadcast_to(f, (CHUNK, 1)) for f in final])).astype(F32)
    eg, es = jnp.exp(G - mid), jnp.exp(mid - G)
    eo = jnp.exp(G) * opening
    ex = jnp.exp(last - G) * closing
    kg, qg, ks = (kn * eg).astype(BF), (qn * eg).astype(BF), (kn * es).astype(BF)
    kout = (kn * ex).astype(BF)
    ap = mm(cat([kg, qg]), ks, 1, 1)
    a = jnp.where(strict, ap[:128], 0.0)
    p = jnp.where(causal, ap[128:], 0.0).astype(BF)
    t = invert(beta * a, i, j).astype(BF)
    uw = mm(t, cat([beta * v, beta * (kn * eo)], 1))
    u, w = uw[:, :128], uw[:, 128:]
    qt = qn * eo - mm(p, w)
    tk = mm(t, kout, 0, 0)
    pt = mm(p, t)
    for h, s in enumerate(HEADS):
        end = CHUNK * h + CHUNK - 1
        keep = jnp.exp(G[end : end + 1]) * (final[h] == 0).astype(F32)
        passed[c, h : h + 1, :] = keep
        kw = mm(kout[s], uw[s], 0, 0)
        chain[c, h, 0] = jnp.where(i == j, keep, 0.0) - kw[:, 128:]
        chain[c, h, 1] = kw[:, :128]
    wide = lambda z: jnp.broadcast_to(z, (128, 128))
    for slot, value in (
        (QN, qn), (KN, kn), (RQ, wide(rq)), (RK, wide(rk)), (EO, eo), (EG, eg), (ES, es),
        (EX, ex), (U_, u), (BETA, wide(beta)),
    ):
        sf[c, slot] = value
    for slot, value in (
        (QG, qg), (KG, kg), (KS, ks), (W_, w), (TK, tk), (KO, kout), (PT, pt),
        (CAUSAL, causal.astype(F32)), (STRICT, strict.astype(F32)),
    ):
        sb[c, slot] = value.astype(BF)
    return qt


def second_pass(c, S, dO, sf, sb):
    S = [s.astype(BF) for s in S]
    dO = dO.astype(BF)
    w = sb[c, W_]
    x = sf[c, U_] - cat([mm(w[s], S[h]) for h, s in enumerate(HEADS)])
    xb = x.astype(BF)
    dp = jnp.where(sb[c, CAUSAL].astype(F32) > 0, mm(dO, xb, 1, 1), 0.0).astype(BF)
    qs = cat([mm(dO[s], S[h], 1, 1) for h, s in enumerate(HEADS)]) * sf[c, EO]
    dqg = mm(dp, sb[c, KS])
    dks = mm(dp, sb[c, QG], 0, 0)
    y0 = mm(sb[c, PT], dO, 0, 0)
    return S, x, xb, qs, dqg, dks, y0


def third_pass(c, kept, D, sf, sb, passed):
    f = lambda slot: sf[c, slot]
    b = lambda slot: sb[c, slot]
    i, j = iotas()
    S, x, xb, qs, dqg, dks, y0 = kept
    D = [d.astype(BF) for d in D]
    tk, beta, eo = b(TK), f(BETA), f(EO)
    y = y0 + cat([mm(tk[s], D[h]) for h, s in enumerate(HEADS)])
    dbeta = rowsum(y * x) / beta[:, :1]
    dv = beta * y
    yb = y.astype(BF)
    da = jnp.where(b(STRICT).astype(F32) > 0, -beta * mm(yb, xb, 1, 1), 0.0).astype(BF)
    ke = cat([mm(yb[s], S[h], 1, 1) for h, s in enumerate(HEADS)]) * (-beta * eo)
    dko = cat([mm(xb[s], D[h], 1, 1) for h, s in enumerate(HEADS)])
    qg, kg, ks = b(QG), b(KG), b(KS)
    dkg = mm(da, ks)
    dks = dks + mm(da, kg, 0, 0)
    qn, kn, eg = f(QN), f(KN), f(EG)
    dq = qs + dqg * eg
    dk = ke + dkg * eg + dks * f(ES) + dko * f(EX)
    kd = b(KO).astype(F32) * dko
    dG = (
        qn * qs + qg.astype(F32) * dqg + kg.astype(F32) * dkg
        - ks.astype(F32) * dks + kn * ke - kd
    )
    ends = []
    for h, s in enumerate(HEADS):
        hi, lo = split(S[h].astype(F32) * D[h].astype(F32))
        through = mm(jnp.ones((8, 256), BF), cat([hi, lo], 1), 1, 1)[0:1]
        ends.append(jnp.sum(kd[s], axis=0, keepdims=True) + passed[c, h : h + 1, :] * through)
    hi, lo = split(dG)
    upper = (((i >> 6) == (j >> 6)) & (i <= j)).astype(BF)
    dg = mm(cat([upper, upper], 1), cat([hi, lo])) + per_head(ends)
    dqr = f(RQ) * (dq - qn * rowsum(qn * dq))
    dkr = f(RK) * (dk - kn * rowsum(kn * dk))
    return dqr, dkr, dv, dg, dbeta


def kernel(
    x_ref, og_ref, wq_ref, wk_ref, wv_ref, wo_ref, gate_ref, beta_ref, init_ref, ds_ref,
    ig_ref, gg_ref, bg_ref, sg_ref,
    gate, beta_in, start, ds, wcat, wo, wot, xg, raw, gcat, sf, sb, chain, passed, prefix, qe,
    own, heard, comm, states, grads, part, r1, t2, t2f, r2,
    wsem, gsend, grecv, esend, erecv, rsend, rrecv,
):
    seq, head = lax.axis_index("seq"), lax.axis_index("head")
    y, x = head // 4, head % 4
    z, core = seq // 2, seq % 2
    xs = [{"head": y * 4 + (x + o) % 4} for o in (1, 2, 3)]
    ys = [{"head": ((y + o) % 4) * 4 + x} for o in (1, 2, 3)]
    zs = [{"seq": ((z + o) % 4) * 2 + core} for o in (1, 2, 3)]
    sibling = {"seq": z * 2 + (1 - core)}

    loads = [
        pltpu.make_async_copy(
            ref.at[:, 128 * half : 128 * half + 128], xg.at[item, half, y, x], wsem.at[item, half]
        )
        for item, ref in enumerate((x_ref, og_ref))
        for half in (0, 1)
    ]
    loads += [
        pltpu.make_async_copy(ref, wcat.at[:, 256 * n : 256 * n + 256], wsem.at[2, n])
        for n, ref in enumerate((wq_ref, wk_ref, wv_ref))
    ]
    loads += [
        pltpu.make_async_copy(src, dst, wsem.at[3, n])
        for n, (src, dst) in enumerate((
            (wo_ref, wo), (gate_ref, gate), (beta_ref, beta_in), (init_ref, start), (ds_ref, ds)
        ))
    ]
    for load in loads:
        load.start()

    barrier = pltpu.get_barrier_semaphore()
    partners = xs + ys + zs + [sibling]
    for device in partners:
        pl.semaphore_signal(barrier, inc=1, device_id=device, device_id_type=MESH)

    pl.semaphore_wait(barrier, len(partners))

    sent = []
    for load in loads[:4]:
        load.wait()

    def remote(src, dst, ssem, rsem, device):
        copy = pltpu.make_async_remote_copy(
            src_ref=src, dst_ref=dst, send_sem=ssem, recv_sem=rsem,
            device_id=device, device_id_type=MESH,
        )
        sent.append(copy)
        return copy

    def gather(item, half, phase):
        axis = xs if (half + phase) % 2 == 0 else ys
        if phase == 0:
            block = xg.at[item, half, y, x]
        else:
            block = xg.at[item, 0, y] if half == 0 else xg.at[item, 1, :, x]
        return [
            remote(block, block, gsend.at[item, half, phase, o], grecv.at[item, half, phase, o],
                   axis[o])
            for o in (1, 0, 2)
        ]

    near = [[gather(item, half, 0) for half in (0, 1)] for item in (0, 1)]
    far = [[gather(item, half, 1) for half in (0, 1)] for item in (0, 1)]
    for item in (0, 1):
        for o in range(3):
            for half in (0, 1):
                near[item][half][o].start()
    for item in (0, 1):
        for half in (0, 1):
            for copy in near[item][half]:
                copy.wait_recv()
            for copy in far[item][half]:
                copy.start()

    for load in loads[4:]:
        load.wait()
    for n in range(18):
        wot[128 * n : 128 * n + 128, :] = wo[:, 128 * n : 128 * n + 128].T

    def project(item, weight, columns):
        for half in (0, 1):
            for copy in far[item][half]:
                copy.wait_recv()
            rows = xg[item, half].reshape(2304, 128)
            raw[128 * half : 128 * half + 128, columns] = mm(rows, weight[...], 0, 0)

    project(0, wcat, slice(0, 768))

    def stacked(ref, c, first):
        t = slice(CHUNK * c, CHUNK * c + CHUNK)
        return cat([ref[t, first : first + 128], ref[t, first + 128 : first + 256]])

    diagonal = (
        lax.broadcasted_iota(jnp.int32, (CHUNK, CHUNK), 0)
        == lax.broadcasted_iota(jnp.int32, (CHUNK, CHUNK), 1)
    )
    reads = []
    for c in range(CHUNKS):
        t = slice(CHUNK * c, CHUNK * c + CHUNK)
        beta = cat([rowsum(jnp.where(diagonal, beta_in[h : h + 1, t], 0.0)) for h in (0, 1)])
        reads.append(first_pass(
            c, seq * 256 + CHUNK * c,
            stacked(raw, c, 0), stacked(raw, c, 256), stacked(raw, c, 512),
            stacked(gate, c, 0), beta, ds, sf, sb, chain, passed,
        ))

    for h, rows in enumerate(HEADS):
        m, v = chain[0, h, 0], chain[0, h, 1]
        prefix[h, 0, :, :128], prefix[h, 0, :, 128:] = m, v
        for n in (1, 2, 3):
            step = mm(chain[n, h, 0], cat([m, v], 1))
            m, v = step[:, :128], step[:, 128:] + chain[n, h, 1]
            if n < 3:
                prefix[h, n, :, :128], prefix[h, n, :, 128:] = m, v
        own[h, 0], own[h, 1] = m.astype(BF), v.astype(BF)
    swap = remote(
        own.at[1 - core, pl.ds(0, 2)], heard.at[pl.ds(0, 2)], esend.at[0], erecv.at[0], sibling
    )
    swap.start()
    for h, rows in enumerate(HEADS):
        qe[h, 0:CHUNK] = reads[0][rows].astype(BF)
        for n in (1, 2, 3):
            qe[h, CHUNK * n : CHUNK * n + CHUNK] = mm(
                reads[n][rows], prefix[h, n - 1, :, :128]
            ).astype(BF)
    swap.wait_recv()
    first = core == 0
    m0, b0 = [jnp.where(first, own[core, n], heard[n]) for n in (0, 1)]
    m1, b1 = [jnp.where(first, heard[n], own[core, n]) for n in (0, 1)]
    both = mm(m1, cat([m0, b0], 1))
    comm[z, 0] = both[:, :128].astype(BF)
    comm[z, 1] = (both[:, 128:] + b1.astype(F32)).astype(BF)
    spread = [
        remote(comm.at[z, pl.ds(0, 2)], comm.at[z, pl.ds(0, 2)], esend.at[1 + o],
               erecv.at[1 + o], zs[o])
        for o in (1, 0, 2)
    ]
    for copy in spread:
        copy.start()

    project(1, wot, slice(768, 1024))

    for h in (0, 1):
        dO = raw[:, 768 + 128 * h : 896 + 128 * h]
        own[h, 2] = mm(qe[h], dO, 0, 0).astype(BF)
    swap_l = remote(own.at[1 - core, 2], heard.at[2], esend.at[4], erecv.at[4], sibling)
    swap_l.start()

    for copy in spread:
        copy.wait_recv()
    state, entering = start[core], start[core]
    for n in range(3):
        state = mm(comm[n, 0], state) + comm[n, 1].astype(F32)
        entering = jnp.where(z == n + 1, state, entering)
    after = mm(m0, entering) + b0.astype(F32)
    states[2] = jnp.where(first, after, entering).astype(BF)
    give_s = remote(states.at[2], states.at[core], esend.at[5], erecv.at[5], sibling)
    give_s.start()
    states[core] = jnp.where(first, entering, after).astype(BF)

    swap_l.wait_recv()
    l0 = jnp.where(first, own[core, 2], heard[2])
    l1 = jnp.where(first, heard[2], own[core, 2])
    comm[z, 2] = (l0.astype(F32) + mm(m0, l1, 0, 0)).astype(BF)
    spread_l = [
        remote(comm.at[z, 2], comm.at[z, 2], esend.at[6 + o], erecv.at[6 + o], zs[o])
        for o in (1, 0, 2)
    ]
    for copy in spread_l:
        copy.start()

    give_s.wait_recv()
    S = []
    for h in (0, 1):
        s = states[h]
        S.append([s] + [mm(prefix[h, n, :, :128], s) + prefix[h, n, :, 128:] for n in range(3)])
    kept = [
        second_pass(c, [S[0][c], S[1][c]], stacked(raw, c, 768), sf, sb) for c in range(CHUNKS)
    ]
    local = [[None] * CHUNKS, [None] * CHUNKS]
    turn = [[None] * CHUNKS, [None] * CHUNKS]
    for h, rows in enumerate(HEADS):
        for n in (3, 2, 1):
            step = mm(reads[n][rows], stacked(raw, n, 768)[rows], 0, 0)
            m = chain[n, h, 0]
            if n == 3:
                local[h][2], turn[h][2] = step, m.T
            else:
                local[h][n - 1] = mm(m, local[h][n], 0, 0) + step
                turn[h][n - 1] = mm(m, turn[h][n], 0, 0)

    for copy in spread_l:
        copy.wait_recv()
    grad = comm[3, 2].astype(F32)
    leaving = jnp.where(z == 2, grad, 0.0)
    for n in (2, 1, 0):
        grad = mm(comm[n, 0], grad, 0, 0) + comm[n, 2].astype(F32)
        leaving = jnp.where(z == n - 1, grad, leaving)
    before = mm(m1, leaving, 0, 0) + l1.astype(F32)
    grads[2, 0] = jnp.where(first, leaving, before).astype(BF)
    grads[2, 1] = grad.astype(BF)
    give_d = remote(grads.at[2], grads.at[core], esend.at[9], erecv.at[9], sibling)
    give_d.start()
    grads[core, 0] = jnp.where(first, before, leaving).astype(BF)
    grads[core, 1] = grad.astype(BF)
    give_d.wait_recv()

    D = []
    for h in (0, 1):
        sg_ref[h] = grads[h, 1].astype(F32)
        d = grads[h, 0]
        D.append([mm(turn[h][n], d) + local[h][n] for n in range(3)] + [d])

    def share(half, target):
        rows = gcat[128 * half : 128 * half + 128, :]
        if half == 0:
            return mm(wcat[pl.ds(pl.multiple_of(576 * target, 16), 576), :], rows, 1, 1)
        return cat([
            mm(wcat[pl.ds(pl.multiple_of(576 * n + 144 * target, 16), 144), :], rows, 1, 1)
            for n in range(4)
        ])

    sums = [[], []]
    for half, place, axis in ((0, y, ys), (1, x, xs)):
        for c in (2 * half, 2 * half + 1):
            t = slice(CHUNK * c, CHUNK * c + CHUNK)
            dq, dk, dv, dg, dbeta = third_pass(c, kept[c], [D[0][c], D[1][c]], sf, sb, passed)
            for h, s in enumerate(HEADS):
                for n, value in enumerate((dq, dk, dv)):
                    gcat[t, 256 * n + 128 * h : 256 * n + 128 * h + 128] = value[s].astype(BF)
                gg_ref[t, 128 * h : 128 * h + 128] = dg[s]
                bg_ref[h : h + 1, t] = jnp.sum(
                    jnp.where(diagonal, dbeta[s], 0.0), axis=0, keepdims=True
                )
        for o in (1, 0, 2):
            part[half, o] = share(half, (place + o + 1) % 4).astype(BF)
            copy = remote(
                part.at[half, o], r1.at[half, o], rsend.at[half, 0, o], rrecv.at[half, 0, o],
                axis[o],
            )
            copy.start()
            sums[half].append(copy)
    ends = [[], []]
    totals = [share(0, y), share(1, x)]
    for half, place, axis in ((0, x, xs), (1, y, ys)):
        total = totals[half]
        for copy in sums[half]:
            copy.wait_recv()
        for o in range(3):
            total = total + r1[half, o].astype(F32)
        t2f[half] = total.reshape(4, 144, 128)
        t2[half] = total.astype(BF).reshape(4, 144, 128)
        for o in (1, 0, 2):
            copy = remote(
                t2.at[half, (place + o + 1) % 4], r2.at[half, o],
                rsend.at[half, 1, o], rrecv.at[half, 1, o], axis[o],
            )
            copy.start()
            ends[half].append(copy)
    done = []
    for half, place in ((0, x), (1, y)):
        total = t2f[half, place]
        for copy in ends[half]:
            copy.wait_recv()
        for o in range(3):
            total = total + r2[half, o].astype(F32)
        done.append(total)
    ig_ref[...] = cat(done, 1).astype(BF)

    for copy in sent:
        copy.wait_send()


def finish(*refs):
    for n in range(4):
        refs[4 + n][...] = refs[n][...]


def per_device(inputs, output_grad, *others):
    vmem = pl.BlockSpec(memory_space=pltpu.VMEM)
    anywhere = pl.BlockSpec(memory_space=pl.ANY)
    scratch = lambda *shape, dtype=F32: pltpu.VMEM(shape, dtype)
    dma = lambda *shape: pltpu.SemaphoreType.DMA(shape)
    shapes = (
        jax.ShapeDtypeStruct((144, 256), BF),
        jax.ShapeDtypeStruct((256, 256), F32),
        jax.ShapeDtypeStruct((2, 256), F32),
        jax.ShapeDtypeStruct((2, 128, 128), F32),
    )
    results = pl.pallas_call(
        kernel,
        out_shape=shapes,
        in_specs=[anywhere] * 10,
        out_specs=(vmem,) * 4,
        scratch_shapes=[
            scratch(256, 256),
            scratch(2, 256),
            scratch(2, 128, 128),
            pltpu.SMEM((4,), jnp.int32),
            scratch(2304, 768, dtype=BF),
            scratch(256, 2304, dtype=BF),
            scratch(2304, 256, dtype=BF),
            scratch(2, 2, 4, 4, 144, 128, dtype=BF),
            scratch(256, 1024),
            scratch(256, 768, dtype=BF),
            scratch(CHUNKS, 10, 128, 128),
            scratch(CHUNKS, 9, 128, 128, dtype=BF),
            scratch(CHUNKS, 2, 2, 128, 128),
            scratch(CHUNKS, 8, 128),
            scratch(2, 3, 128, 256),
            scratch(2, 256, 128, dtype=BF),
            scratch(2, 3, 128, 128, dtype=BF),
            scratch(3, 128, 128, dtype=BF),
            scratch(4, 3, 128, 128, dtype=BF),
            scratch(3, 128, 128, dtype=BF),
            scratch(3, 2, 128, 128, dtype=BF),
            scratch(2, 3, 576, 128, dtype=BF),
            scratch(2, 3, 576, 128, dtype=BF),
            scratch(2, 4, 144, 128, dtype=BF),
            scratch(2, 4, 144, 128),
            scratch(2, 3, 144, 128, dtype=BF),
            dma(4, 5), dma(2, 2, 2, 3), dma(2, 2, 2, 3), dma(10), dma(10), dma(2, 2, 3), dma(2, 2, 3),
        ],
        compiler_params=pltpu.CompilerParams(
            collective_id=0, has_side_effects=True, vmem_limit_bytes=60 * 1024 * 1024
        ),
        cost_estimate=pl.CostEstimate(
            flops=3 * 10**9, bytes_accessed=6 * 10**6, transcendentals=3 * 10**5
        ),
    )(inputs.T, output_grad.T, *others)
    results = pl.pallas_call(
        finish,
        out_shape=shapes,
        in_specs=[vmem] * 4,
        out_specs=(vmem,) * 4,
    )(*results)
    return (results[0].T, *results[1:])


def solution(mesh):
    return jax.shard_map(
        per_device,
        mesh=mesh,
        in_specs=(
            P("seq", "head"),
            P("seq", "head"),
            P(None, "head"),
            P(None, "head"),
            P(None, "head"),
            P("head", None),
            P("seq", "head"),
            P("head", "seq"),
            P("head", None, None),
            P(),
        ),
        out_specs=(P("seq", "head"), P("seq", "head"), P("head", "seq"), P("head", None, None)),
        check_vma=False,
    )
```

time: 76 us -> 63 us (0.83)
  local copies, waits for them, and re-layouts: 12.9 us -> 0 us
    unnamed x21 -> x0, local copies, waits for them, and re-layouts: 12.2 us -> none
    pallas_call x1 -> x2, Pallas kernels: 61.7 us -> 61.8 us  [the longest x1 60 us: per_device(): pl.pallas_call(kernel, out_shape=shapes, in_specs=[anywhere] * 10, out_sp...]
where the time goes in v2:
time: 63 us; the launch traced here: 62.4 us
  Pallas kernels  61.8 us (98%)
  between operations  0.64 us (1%)
    pallas_call x1, Pallas kernels, per_device(): pl.pallas_call(kernel, out_shape=shapes, in_specs=[anywhere] * 10, out_sp...  60 us
    pallas_call x1, Pallas kernels, per_device(): pl.pallas_call(finish, out_shape=shapes, in_specs=[vmem] * 4, out_specs=(...  1.81 us

profile of v2, /device:TPU:0, one launch (start us, length us, event | category | flops | bytes accessed | tf_op | source)
XLA Modules:
  0.0 62.4 jit_solution(17889702576969726474)
XLA Ops:
  0.6 60.0 %shard_map.129 = (bf16[144,256]{1,0:T(8,128)(2,1)}, f32[256,256]{1,0:T(8,128)}, f32[2,256]{1,0:T(2,128)}, f32[2,128,128]{2,1,0:T(8,128)}) custom-call(bf16[144,256]{1,0:T(8,128)(2,1)} %bitcast.3, bf16[144,256]{1,0:T(8,128)(2,1)} %bitcast.4, bf16[2304,256]{1,0:T(8,128)(2,1)} %wq_ref.1, bf16[2304,256]{1,0:T(8,128)(2,1)} %wk_ref.1, bf16[2304,256]{1,0:T(8,128)(2,1)} %wv_ref.1, ...), custom_call_target="tpu_custom_call" | custom-call | flops 3000000000 | bytes 6000000 | tf_op jit(solution)/shard_map/pallas_call | solution.py:475
  60.6 1.8 %shard_map.130 = (bf16[144,256]{1,0:T(8,128)(2,1)}, f32[256,256]{1,0:T(8,128)}, f32[2,256]{1,0:T(2,128)}, f32[2,128,128]{2,1,0:T(8,128)}) custom-call(bf16[144,256]{1,0:T(8,128)(2,1)} %get-tuple-element.12.refs_0_, f32[256,256]{1,0:T(8,128)} %get-tuple-element.13.refs_1_, f32[2,256]{1,0:T(2,128)} %get-tuple-element.14.refs_2_, ...), custom_call_target="tpu_custom_call" | custom-call | tf_op jit(solution)/shard_map/pallas_call | solution.py:516

commit v3 on v2

--- a/solution.py
+++ b/solution.py
@@ -18,6 +18,11 @@
     )
 
 
+def mm3(a, b, ca=1, cb=0):
+    (ah, al), (bh, bl) = split(a), split(b)
+    return mm(ah, bh, ca, cb) + (mm(ah, bl, ca, cb) + mm(al, bh, ca, cb))
+
+
 def cat(parts, axis=0):
     return jnp.concatenate(parts, axis=axis)
 
@@ -44,18 +49,38 @@
 HEADS = (slice(0, CHUNK), slice(CHUNK, 2 * CHUNK))
 
 
+def together(steps):
+    results = [None] * len(steps)
+    live = list(range(len(steps)))
+    while live:
+        for n in list(live):
+            try:
+                next(steps[n])
+            except StopIteration as stop:
+                results[n] = stop.value
+                live.remove(n)
+    return results
+
+
 def invert(n, i, j):
     eye = (i == j).astype(F32)
     d = jnp.where((i >> 4) == (j >> 4), n, 0.0)
     d2 = mm(d, d)
+    yield
     p = mm(eye - d, eye + d2)
     d4 = mm(d2, d2)
+    yield
     p = mm(p, eye + d4)
     d8 = mm(d4, d4)
+    yield
     t = mm(p, eye + d8)
+    yield
     for s in (4, 5):
         off = jnp.where(((i >> (s + 1)) == (j >> (s + 1))) & ((i >> s) != (j >> s)), n, 0.0)
-        t = t - mm(t, mm(off, t))
+        step = mm(off, t)
+        yield
+        t = t - mm(t, step)
+        yield
     return t
 
 
@@ -86,6 +111,7 @@
     qn, kn = q * rq, k * rk
     hi, lo = split(g)
     G = mm(cat([tri, tri], 1), cat([hi, lo]))
+    yield
     mid = per_head([G[31:32], G[95:96]])
     last = per_head([G[63:64], G[127:128]])
     opening = (segr == 0).astype(F32)
@@ -95,21 +121,26 @@
     eo = jnp.exp(G) * opening
     ex = jnp.exp(last - G) * closing
     kg, qg, ks = (kn * eg).astype(BF), (qn * eg).astype(BF), (kn * es).astype(BF)
-    kout = (kn * ex).astype(BF)
+    kof = kn * ex
+    kout = kof.astype(BF)
+    yield
     ap = mm(cat([kg, qg]), ks, 1, 1)
+    yield
     a = jnp.where(strict, ap[:128], 0.0)
     p = jnp.where(causal, ap[128:], 0.0).astype(BF)
-    t = invert(beta * a, i, j).astype(BF)
+    t = (yield from invert(beta * a, i, j)).astype(BF)
     uw = mm(t, cat([beta * v, beta * (kn * eo)], 1))
+    yield
     u, w = uw[:, :128], uw[:, 128:]
     qt = qn * eo - mm(p, w)
     tk = mm(t, kout, 0, 0)
     pt = mm(p, t)
+    yield
     for h, s in enumerate(HEADS):
         end = CHUNK * h + CHUNK - 1
         keep = jnp.exp(G[end : end + 1]) * (final[h] == 0).astype(F32)
         passed[c, h : h + 1, :] = keep
-        kw = mm(kout[s], uw[s], 0, 0)
+        kw = mm3(kof[s], uw[s], 0, 0)
         chain[c, h, 0] = jnp.where(i == j, keep, 0.0) - kw[:, 128:]
         chain[c, h, 1] = kw[:, :128]
     wide = lambda z: jnp.broadcast_to(z, (128, 128))
@@ -132,38 +163,50 @@
     w = sb[c, W_]
     x = sf[c, U_] - cat([mm(w[s], S[h]) for h, s in enumerate(HEADS)])
     xb = x.astype(BF)
+    yield
     dp = jnp.where(sb[c, CAUSAL].astype(F32) > 0, mm(dO, xb, 1, 1), 0.0).astype(BF)
     qs = cat([mm(dO[s], S[h], 1, 1) for h, s in enumerate(HEADS)]) * sf[c, EO]
+    yield
     dqg = mm(dp, sb[c, KS])
     dks = mm(dp, sb[c, QG], 0, 0)
     y0 = mm(sb[c, PT], dO, 0, 0)
-    return S, x, xb, qs, dqg, dks, y0
-
-
-def third_pass(c, kept, D, sf, sb, passed):
+    yield
+    qn = sf[c, QN]
+    dq = qs + dqg * sf[c, EG]
+    dqr = sf[c, RQ] * (dq - qn * rowsum(qn * dq))
+    gate = qn * qs + sb[c, QG].astype(F32) * dqg
+    return dqr, (S, x, xb, gate, dks, y0)
+
+
+def third_pass(c, kept, D, sf, sb):
     f = lambda slot: sf[c, slot]
     b = lambda slot: sb[c, slot]
-    i, j = iotas()
-    S, x, xb, qs, dqg, dks, y0 = kept
+    S, x, xb, gate, dks, y0 = kept
     D = [d.astype(BF) for d in D]
     tk, beta, eo = b(TK), f(BETA), f(EO)
     y = y0 + cat([mm(tk[s], D[h]) for h, s in enumerate(HEADS)])
-    dbeta = rowsum(y * x) / beta[:, :1]
-    dv = beta * y
     yb = y.astype(BF)
+    yield
     da = jnp.where(b(STRICT).astype(F32) > 0, -beta * mm(yb, xb, 1, 1), 0.0).astype(BF)
     ke = cat([mm(yb[s], S[h], 1, 1) for h, s in enumerate(HEADS)]) * (-beta * eo)
     dko = cat([mm(xb[s], D[h], 1, 1) for h, s in enumerate(HEADS)])
-    qg, kg, ks = b(QG), b(KG), b(KS)
-    dkg = mm(da, ks)
-    dks = dks + mm(da, kg, 0, 0)
-    qn, kn, eg = f(QN), f(KN), f(EG)
-    dq = qs + dqg * eg
-    dk = ke + dkg * eg + dks * f(ES) + dko * f(EX)
-    kd = b(KO).astype(F32) * dko
+    yield
+    dkg = mm(da, b(KS))
+    dks = dks + mm(da, b(KG), 0, 0)
+    yield
+    kn = f(KN)
+    dk = ke + dkg * f(EG) + dks * f(ES) + dko * f(EX)
+    dkr = f(RK) * (dk - kn * rowsum(kn * dk))
+    return dkr, beta * y, (S, D, x, y, gate, ke, dko, dkg, dks)
+
+
+def last_pass(c, kept, sf, sb, passed):
+    i, j = iotas()
+    S, D, x, y, gate, ke, dko, dkg, dks = kept
+    dbeta = rowsum(y * x) / sf[c, BETA][:, :1]
+    kd = sb[c, KO].astype(F32) * dko
     dG = (
-        qn * qs + qg.astype(F32) * dqg + kg.astype(F32) * dkg
-        - ks.astype(F32) * dks + kn * ke - kd
+        gate + sb[c, KG].astype(F32) * dkg - sb[c, KS].astype(F32) * dks + sf[c, KN] * ke - kd
     )
     ends = []
     for h, s in enumerate(HEADS):
@@ -172,10 +215,10 @@
         ends.append(jnp.sum(kd[s], axis=0, keepdims=True) + passed[c, h : h + 1, :] * through)
     hi, lo = split(dG)
     upper = (((i >> 6) == (j >> 6)) & (i <= j)).astype(BF)
+    yield
     dg = mm(cat([upper, upper], 1), cat([hi, lo])) + per_head(ends)
-    dqr = f(RQ) * (dq - qn * rowsum(qn * dq))
-    dkr = f(RK) * (dk - kn * rowsum(kn * dk))
-    return dqr, dkr, dv, dg, dbeta
+    yield
+    return dg, dbeta
 
 
 def kernel(
@@ -279,25 +322,34 @@
         lax.broadcasted_iota(jnp.int32, (CHUNK, CHUNK), 0)
         == lax.broadcasted_iota(jnp.int32, (CHUNK, CHUNK), 1)
     )
-    reads = []
-    for c in range(CHUNKS):
-        t = slice(CHUNK * c, CHUNK * c + CHUNK)
-        beta = cat([rowsum(jnp.where(diagonal, beta_in[h : h + 1, t], 0.0)) for h in (0, 1)])
-        reads.append(first_pass(
+    betas = [
+        cat([
+            rowsum(jnp.where(diagonal, beta_in[h : h + 1, CHUNK * c : CHUNK * c + CHUNK], 0.0))
+            for h in (0, 1)
+        ])
+        for c in range(CHUNKS)
+    ]
+    reads = together([
+        first_pass(
             c, seq * 256 + CHUNK * c,
             stacked(raw, c, 0), stacked(raw, c, 256), stacked(raw, c, 512),
-            stacked(gate, c, 0), beta, ds, sf, sb, chain, passed,
-        ))
-
-    for h, rows in enumerate(HEADS):
-        m, v = chain[0, h, 0], chain[0, h, 1]
-        prefix[h, 0, :, :128], prefix[h, 0, :, 128:] = m, v
-        for n in (1, 2, 3):
-            step = mm(chain[n, h, 0], cat([m, v], 1))
-            m, v = step[:, :128], step[:, 128:] + chain[n, h, 1]
+            stacked(gate, c, 0), betas[c], ds, sf, sb, chain, passed,
+        )
+        for c in range(CHUNKS)
+    ])
+
+    pairs = [(chain[0, h, 0], chain[0, h, 1]) for h in (0, 1)]
+    for n in range(CHUNKS):
+        for h in (0, 1):
+            m, v = pairs[h]
+            if n > 0:
+                step = mm3(chain[n, h, 0], cat([m, v], 1))
+                m, v = step[:, :128], step[:, 128:] + chain[n, h, 1]
             if n < 3:
                 prefix[h, n, :, :128], prefix[h, n, :, 128:] = m, v
-        own[h, 0], own[h, 1] = m.astype(BF), v.astype(BF)
+            else:
+                own[h, 0], own[h, 1] = m.astype(BF), v.astype(BF)
+            pairs[h] = m, v
     swap = remote(
         own.at[1 - core, pl.ds(0, 2)], heard.at[pl.ds(0, 2)], esend.at[0], erecv.at[0], sibling
     )
@@ -331,6 +383,17 @@
     swap_l = remote(own.at[1 - core, 2], heard.at[2], esend.at[4], erecv.at[4], sibling)
     swap_l.start()
 
+    swap_l.wait_recv()
+    l0 = jnp.where(first, own[core, 2], heard[2])
+    l1 = jnp.where(first, heard[2], own[core, 2])
+    comm[z, 2] = (l0.astype(F32) + mm(m0, l1, 0, 0)).astype(BF)
+    spread_l = [
+        remote(comm.at[z, 2], comm.at[z, 2], esend.at[6 + o], erecv.at[6 + o], zs[o])
+        for o in (1, 0, 2)
+    ]
+    for copy in spread_l:
+        copy.start()
+
     for copy in spread:
         copy.wait_recv()
     state, entering = start[core], start[core]
@@ -343,36 +406,17 @@
     give_s.start()
     states[core] = jnp.where(first, entering, after).astype(BF)
 
-    swap_l.wait_recv()
-    l0 = jnp.where(first, own[core, 2], heard[2])
-    l1 = jnp.where(first, heard[2], own[core, 2])
-    comm[z, 2] = (l0.astype(F32) + mm(m0, l1, 0, 0)).astype(BF)
-    spread_l = [
-        remote(comm.at[z, 2], comm.at[z, 2], esend.at[6 + o], erecv.at[6 + o], zs[o])
-        for o in (1, 0, 2)
-    ]
-    for copy in spread_l:
-        copy.start()
-
-    give_s.wait_recv()
-    S = []
-    for h in (0, 1):
-        s = states[h]
-        S.append([s] + [mm(prefix[h, n, :, :128], s) + prefix[h, n, :, 128:] for n in range(3)])
-    kept = [
-        second_pass(c, [S[0][c], S[1][c]], stacked(raw, c, 768), sf, sb) for c in range(CHUNKS)
-    ]
     local = [[None] * CHUNKS, [None] * CHUNKS]
     turn = [[None] * CHUNKS, [None] * CHUNKS]
-    for h, rows in enumerate(HEADS):
-        for n in (3, 2, 1):
+    for n in (3, 2, 1):
+        for h, rows in enumerate(HEADS):
             step = mm(reads[n][rows], stacked(raw, n, 768)[rows], 0, 0)
             m = chain[n, h, 0]
             if n == 3:
                 local[h][2], turn[h][2] = step, m.T
             else:
-                local[h][n - 1] = mm(m, local[h][n], 0, 0) + step
-                turn[h][n - 1] = mm(m, turn[h][n], 0, 0)
+                local[h][n - 1] = mm3(m, local[h][n], 0, 0) + step
+                turn[h][n - 1] = mm3(m, turn[h][n], 0, 0)
 
     for copy in spread_l:
         copy.wait_recv()
@@ -388,6 +432,24 @@
     give_d.start()
     grads[core, 0] = jnp.where(first, before, leaving).astype(BF)
     grads[core, 1] = grad.astype(BF)
+    give_s.wait_recv()
+    S = []
+    for h in (0, 1):
+        s = states[h]
+        S.append([s] + [mm(prefix[h, n, :, :128], s) + prefix[h, n, :, 128:] for n in range(3)])
+    outs = together([
+        second_pass(c, [S[0][c], S[1][c]], stacked(raw, c, 768), sf, sb) for c in range(CHUNKS)
+    ])
+    kept = [rest for _, rest in outs]
+
+    def keep_rows(c, first, value):
+        for h, s in enumerate(HEADS):
+            gcat[CHUNK * c : CHUNK * c + CHUNK, first + 128 * h : first + 128 * h + 128] = value[
+                s
+            ].astype(BF)
+
+    for c, (dqr, _) in enumerate(outs):
+        keep_rows(c, 0, dqr)
     give_d.wait_recv()
 
     D = []
@@ -405,19 +467,15 @@
             for n in range(4)
         ])
 
+    outs = together([
+        third_pass(c, kept[c], [D[0][c], D[1][c]], sf, sb) for c in range(CHUNKS)
+    ])
+    for c, (dkr, dv, _) in enumerate(outs):
+        keep_rows(c, 256, dkr)
+        keep_rows(c, 512, dv)
     sums = [[], []]
-    for half, place, axis in ((0, y, ys), (1, x, xs)):
-        for c in (2 * half, 2 * half + 1):
-            t = slice(CHUNK * c, CHUNK * c + CHUNK)
-            dq, dk, dv, dg, dbeta = third_pass(c, kept[c], [D[0][c], D[1][c]], sf, sb, passed)
-            for h, s in enumerate(HEADS):
-                for n, value in enumerate((dq, dk, dv)):
-                    gcat[t, 256 * n + 128 * h : 256 * n + 128 * h + 128] = value[s].astype(BF)
-                gg_ref[t, 128 * h : 128 * h + 128] = dg[s]
-                bg_ref[h : h + 1, t] = jnp.sum(
-                    jnp.where(diagonal, dbeta[s], 0.0), axis=0, keepdims=True
-                )
-        for o in (1, 0, 2):
+    for o in (1, 0, 2):
+        for half, place, axis in ((0, y, ys), (1, x, xs)):
             part[half, o] = share(half, (place + o + 1) % 4).astype(BF)
             copy = remote(
                 part.at[half, o], r1.at[half, o], rsend.at[half, 0, o], rrecv.at[half, 0, o],
@@ -425,6 +483,15 @@
             )
             copy.start()
             sums[half].append(copy)
+    for c, (dg, dbeta) in enumerate(together([
+        last_pass(c, outs[c][2], sf, sb, passed) for c in range(CHUNKS)
+    ])):
+        t = slice(CHUNK * c, CHUNK * c + CHUNK)
+        for h, s in enumerate(HEADS):
+            gg_ref[t, 128 * h : 128 * h + 128] = dg[s]
+            bg_ref[h : h + 1, t] = jnp.sum(
+                jnp.where(diagonal, dbeta[s], 0.0), axis=0, keepdims=True
+            )
     ends = [[], []]
     totals = [share(0, y), share(1, x)]
     for half, place, axis in ((0, x, xs), (1, y, ys)):

time: 63 us -> 55 us (0.87)
  Pallas kernels: 61.8 us -> 53.4 us
    pallas_call x1, Pallas kernels: 60 us -> 51.6 us  [per_device(): pl.pallas_call(kernel, out_shape=shapes, in_specs=[anywhere] * 10, out_sp...]
where the time goes in v3:
time: 55 us; the launch traced here: 54 us
  Pallas kernels  53.4 us (97%)
  between operations  0.64 us (1%)
    pallas_call x1, Pallas kernels, per_device(): pl.pallas_call(kernel, out_shape=shapes, in_specs=[anywhere] * 10, out_sp...  51.6 us
    pallas_call x1, Pallas kernels, per_device(): pl.pallas_call(finish, out_shape=shapes, in_specs=[vmem] * 4, out_specs=(...  1.81 us

profile of v3, /device:TPU:0, one launch (start us, length us, event | category | flops | bytes accessed | tf_op | source)
XLA Modules:
  0.0 54.0 jit_solution(2354215843464479968)
XLA Ops:
  0.6 51.6 %shard_map.129 = (bf16[144,256]{1,0:T(8,128)(2,1)}, f32[256,256]{1,0:T(8,128)}, f32[2,256]{1,0:T(2,128)}, f32[2,128,128]{2,1,0:T(8,128)}) custom-call(bf16[144,256]{1,0:T(8,128)(2,1)} %bitcast.3, bf16[144,256]{1,0:T(8,128)(2,1)} %bitcast.4, bf16[2304,256]{1,0:T(8,128)(2,1)} %wq_ref.1, bf16[2304,256]{1,0:T(8,128)(2,1)} %wk_ref.1, bf16[2304,256]{1,0:T(8,128)(2,1)} %wv_ref.1, ...), custom_call_target="tpu_custom_call" | custom-call | flops 3000000000 | bytes 6000000 | tf_op jit(solution)/shard_map/pallas_call | solution.py:542
  52.2 1.8 %shard_map.130 = (bf16[144,256]{1,0:T(8,128)(2,1)}, f32[256,256]{1,0:T(8,128)}, f32[2,256]{1,0:T(2,128)}, f32[2,128,128]{2,1,0:T(8,128)}) custom-call(bf16[144,256]{1,0:T(8,128)(2,1)} %get-tuple-element.12.refs_0_, f32[256,256]{1,0:T(8,128)} %get-tuple-element.13.refs_1_, f32[2,256]{1,0:T(2,128)} %get-tuple-element.14.refs_2_, ...), custom_call_target="tpu_custom_call" | custom-call | tf_op jit(solution)/shard_map/pallas_call | solution.py:583

commit v4 on v3

--- a/solution.py
+++ b/solution.py
@@ -49,10 +49,14 @@
 HEADS = (slice(0, CHUNK), slice(CHUNK, 2 * CHUNK))
 
 
-def together(steps):
+def together(steps, hooks=None):
+    rounds, hooks = 0, hooks or {}
     results = [None] * len(steps)
     live = list(range(len(steps)))
     while live:
+        if rounds in hooks:
+            hooks[rounds]()
+        rounds += 1
         for n in list(live):
             try:
                 next(steps[n])
@@ -85,7 +89,7 @@
 
 
 (QN, KN, RQ, RK, EO, EG, ES, EX, U_, BETA) = range(10)
-(QG, KG, KS, W_, TK, KO, PT, CAUSAL, STRICT) = range(9)
+(QG, KG, KS, W_, TK, KO, PT, CAUSAL, STRICT, TT) = range(10)
 
 
 def segments(ds_ref, t0):
@@ -100,17 +104,16 @@
     return segr, segc
 
 
-def first_pass(c, t0, q, k, v, g, beta, ds_ref, sf, sb, chain, passed):
+def key_pass(c, t0, k, v, g, beta, ds_ref, sf, sb, chain, passed):
     i, j = iotas()
     segr, segc = segments(ds_ref, t0)
     same = ((i >> 6) == (j >> 6)) & (segr == segc)
     strict, causal = same & (i > j), same & (i >= j)
     tri = (((i >> 6) == (j >> 6)) & (i >= j)).astype(BF)
-    rq = lax.rsqrt(rowsum(q * q) + EPSILON)
-    rk = lax.rsqrt(rowsum(k * k) + EPSILON)
-    qn, kn = q * rq, k * rk
     hi, lo = split(g)
     G = mm(cat([tri, tri], 1), cat([hi, lo]))
+    rk = lax.rsqrt(rowsum(k * k) + EPSILON)
+    kn = k * rk
     yield
     mid = per_head([G[31:32], G[95:96]])
     last = per_head([G[63:64], G[127:128]])
@@ -118,24 +121,16 @@
     final = [segr[63:64], segr[127:128]]
     closing = (segr == cat([jnp.broadcast_to(f, (CHUNK, 1)) for f in final])).astype(F32)
     eg, es = jnp.exp(G - mid), jnp.exp(mid - G)
+    kg, ks = (kn * eg).astype(BF), (kn * es).astype(BF)
+    a = mm(kg, ks, 1, 1)
+    yield
     eo = jnp.exp(G) * opening
     ex = jnp.exp(last - G) * closing
-    kg, qg, ks = (kn * eg).astype(BF), (qn * eg).astype(BF), (kn * es).astype(BF)
     kof = kn * ex
-    kout = kof.astype(BF)
-    yield
-    ap = mm(cat([kg, qg]), ks, 1, 1)
-    yield
-    a = jnp.where(strict, ap[:128], 0.0)
-    p = jnp.where(causal, ap[128:], 0.0).astype(BF)
-    t = (yield from invert(beta * a, i, j)).astype(BF)
+    t = (yield from invert(beta * jnp.where(strict, a, 0.0), i, j)).astype(BF)
     uw = mm(t, cat([beta * v, beta * (kn * eo)], 1))
     yield
     u, w = uw[:, :128], uw[:, 128:]
-    qt = qn * eo - mm(p, w)
-    tk = mm(t, kout, 0, 0)
-    pt = mm(p, t)
-    yield
     for h, s in enumerate(HEADS):
         end = CHUNK * h + CHUNK - 1
         keep = jnp.exp(G[end : end + 1]) * (final[h] == 0).astype(F32)
@@ -145,15 +140,31 @@
         chain[c, h, 1] = kw[:, :128]
     wide = lambda z: jnp.broadcast_to(z, (128, 128))
     for slot, value in (
-        (QN, qn), (KN, kn), (RQ, wide(rq)), (RK, wide(rk)), (EO, eo), (EG, eg), (ES, es),
-        (EX, ex), (U_, u), (BETA, wide(beta)),
+        (KN, kn), (RK, wide(rk)), (EO, eo), (EG, eg), (ES, es), (EX, ex), (U_, u),
+        (BETA, wide(beta)),
     ):
         sf[c, slot] = value
     for slot, value in (
-        (QG, qg), (KG, kg), (KS, ks), (W_, w), (TK, tk), (KO, kout), (PT, pt),
+        (KG, kg), (KS, ks), (W_, w), (KO, kof), (TT, t),
         (CAUSAL, causal.astype(F32)), (STRICT, strict.astype(F32)),
     ):
         sb[c, slot] = value.astype(BF)
+
+
+def query_pass(c, q, sf, sb):
+    rq = lax.rsqrt(rowsum(q * q) + EPSILON)
+    qn = q * rq
+    qg = (qn * sf[c, EG]).astype(BF)
+    p = mm(qg, sb[c, KS], 1, 1)
+    t = sb[c, TT]
+    tk = mm(t, sb[c, KO], 0, 0)
+    yield
+    p = jnp.where(sb[c, CAUSAL].astype(F32) > 0, p, 0.0).astype(BF)
+    qt = qn * sf[c, EO] - mm(p, sb[c, W_])
+    pt = mm(p, t)
+    yield
+    sf[c, QN], sf[c, RQ] = qn, jnp.broadcast_to(rq, (128, 128))
+    sb[c, QG], sb[c, PT], sb[c, TK] = qg, pt.astype(BF), tk.astype(BF)
     return qt
 
 
@@ -169,22 +180,21 @@
     yield
     dqg = mm(dp, sb[c, KS])
     dks = mm(dp, sb[c, QG], 0, 0)
-    y0 = mm(sb[c, PT], dO, 0, 0)
     yield
     qn = sf[c, QN]
     dq = qs + dqg * sf[c, EG]
     dqr = sf[c, RQ] * (dq - qn * rowsum(qn * dq))
     gate = qn * qs + sb[c, QG].astype(F32) * dqg
-    return dqr, (S, x, xb, gate, dks, y0)
-
-
-def third_pass(c, kept, D, sf, sb):
+    return dqr, (S, x, xb, gate, dks)
+
+
+def third_pass(c, kept, y0, tk, d, D, sf, sb):
     f = lambda slot: sf[c, slot]
     b = lambda slot: sb[c, slot]
-    S, x, xb, gate, dks, y0 = kept
-    D = [d.astype(BF) for d in D]
-    tk, beta, eo = b(TK), f(BETA), f(EO)
-    y = y0 + cat([mm(tk[s], D[h]) for h, s in enumerate(HEADS)])
+    S, x, xb, gate, dks = kept
+    beta, eo = f(BETA), f(EO)
+    y = y0 + cat([mm(tk[s], d[h]) for h, s in enumerate(HEADS)])
+    D = [z.astype(BF) for z in D]
     yb = y.astype(BF)
     yield
     da = jnp.where(b(STRICT).astype(F32) > 0, -beta * mm(yb, xb, 1, 1), 0.0).astype(BF)
@@ -225,7 +235,7 @@
     x_ref, og_ref, wq_ref, wk_ref, wv_ref, wo_ref, gate_ref, beta_ref, init_ref, ds_ref,
     ig_ref, gg_ref, bg_ref, sg_ref,
     gate, beta_in, start, ds, wcat, wo, wot, xg, raw, gcat, sf, sb, chain, passed, prefix, qe,
-    own, heard, comm, states, grads, part, r1, t2, t2f, r2,
+    own, heard, comm, states, grads, origin, part, r1, t2, t2f, r2,
     wsem, gsend, grecv, esend, erecv, rsend, rrecv,
 ):
     seq, head = lax.axis_index("seq"), lax.axis_index("head")
@@ -275,44 +285,105 @@
         sent.append(copy)
         return copy
 
-    def gather(item, half, phase):
-        axis = xs if (half + phase) % 2 == 0 else ys
-        if phase == 0:
-            block = xg.at[item, half, y, x]
-        else:
-            block = xg.at[item, 0, y] if half == 0 else xg.at[item, 1, :, x]
+    def near(item, half):
+        block = xg.at[item, half, y, x]
+        axis = xs if half == 0 else ys
         return [
-            remote(block, block, gsend.at[item, half, phase, o], grecv.at[item, half, phase, o],
-                   axis[o])
+            remote(block, block, gsend.at[item, half, o], grecv.at[item, half, o], axis[o])
             for o in (1, 0, 2)
         ]
 
-    near = [[gather(item, half, 0) for half in (0, 1)] for item in (0, 1)]
-    far = [[gather(item, half, 1) for half in (0, 1)] for item in (0, 1)]
-    for item in (0, 1):
+    def piece(item, half, group, n):
+        pair = pl.ds(2 * n, 2)
+        return xg.at[item, 0, group, pair] if half == 0 else xg.at[item, 1, pair, group]
+
+    def far(item, half):
+        place, axis = (y, ys) if half == 0 else (x, xs)
+        copies = []
+        for n, (forward, number) in enumerate(((0, 0), (2, 1), (0, 1), (2, 0))):
+            block = piece(item, half, place, number)
+            copies.append(remote(
+                block, block, gsend.at[item, half, 3 + n], grecv.at[item, half, 3 + n],
+                axis[forward],
+            ))
+        return copies
+
+    def hand_on(item, half):
+        place, axis = (y, ys) if half == 0 else (x, xs)
+        copies = []
+        for n, (forward, group) in enumerate(((0, (place + 3) % 4), (2, (place + 1) % 4))):
+            block = piece(item, half, group, n)
+            copies.append(remote(
+                block, block, gsend.at[item, half, 7 + n], grecv.at[item, half, 7 + n],
+                axis[forward],
+            ))
+        return copies
+
+    parts = [(item, half) for item in (0, 1) for half in (0, 1)]
+    nears = {part: near(*part) for part in parts}
+    fars = {part: far(*part) for part in parts}
+    relays = {part: hand_on(*part) for part in parts}
+
+    def begin(item):
         for o in range(3):
             for half in (0, 1):
-                near[item][half][o].start()
-    for item in (0, 1):
+                nears[item, half][o].start()
+
+    def widen(item):
         for half in (0, 1):
-            for copy in near[item][half]:
+            for copy in nears[item, half]:
                 copy.wait_recv()
-            for copy in far[item][half]:
-                copy.start()
-
+        for n in range(4):
+            for half in (0, 1):
+                fars[item, half][n].start()
+
+    def pass_on(item):
+        for n in (0, 1):
+            for half in (0, 1):
+                fars[item, half][n].wait_recv()
+                relays[item, half][n].start()
+
+    def project(item, weight, taken, columns, groups):
+        for half, place in ((0, y), (1, x)):
+            rows = slice(128 * half, 128 * half + 128)
+            for o in groups:
+                group = (place + o) % 4
+                if half == 0:
+                    block = xg[item, 0, group].reshape(576, 128)
+                    matrix = weight[pl.ds(pl.multiple_of(576 * group, 16), 576), taken]
+                else:
+                    block = cat([xg[item, 1, k, group] for k in range(4)])
+                    matrix = cat([
+                        weight[pl.ds(pl.multiple_of(576 * k + 144 * group, 16), 144), taken]
+                        for k in range(4)
+                    ])
+                value = mm(block, matrix, 0, 0)
+                if o == 0:
+                    raw[rows, columns] = value
+                else:
+                    raw[rows, columns] += value
+
+    begin(0)
+    begin(1)
+    widen(0)
     for load in loads[4:]:
         load.wait()
+    first_rows = (0, wcat, slice(0, 768), slice(0, 768))
+    second_rows = (1, wot, slice(0, 256), slice(768, 1024))
+    project(*first_rows, (0,))
+    pass_on(0)
+    widen(1)
     for n in range(18):
         wot[128 * n : 128 * n + 128, :] = wo[:, 128 * n : 128 * n + 128].T
-
-    def project(item, weight, columns):
-        for half in (0, 1):
-            for copy in far[item][half]:
-                copy.wait_recv()
-            rows = xg[item, half].reshape(2304, 128)
-            raw[128 * half : 128 * half + 128, columns] = mm(rows, weight[...], 0, 0)
-
-    project(0, wcat, slice(0, 768))
+    for half in (0, 1):
+        for copy in fars[0, half][2:]:
+            copy.wait_recv()
+    project(*first_rows, (1, 3))
+    project(*second_rows, (0,))
+    for half in (0, 1):
+        for copy in relays[0, half]:
+            copy.wait_recv()
+    project(0, wcat, slice(256, 768), slice(256, 768), (2,))
 
     def stacked(ref, c, first):
         t = slice(CHUNK * c, CHUNK * c + CHUNK)
@@ -329,41 +400,38 @@
         ])
         for c in range(CHUNKS)
     ]
-    reads = together([
-        first_pass(
-            c, seq * 256 + CHUNK * c,
-            stacked(raw, c, 0), stacked(raw, c, 256), stacked(raw, c, 512),
+    together([
+        key_pass(
+            c, seq * 256 + CHUNK * c, stacked(raw, c, 256), stacked(raw, c, 512),
             stacked(gate, c, 0), betas[c], ds, sf, sb, chain, passed,
         )
         for c in range(CHUNKS)
-    ])
-
-    pairs = [(chain[0, h, 0], chain[0, h, 1]) for h in (0, 1)]
-    for n in range(CHUNKS):
-        for h in (0, 1):
-            m, v = pairs[h]
-            if n > 0:
-                step = mm3(chain[n, h, 0], cat([m, v], 1))
-                m, v = step[:, :128], step[:, 128:] + chain[n, h, 1]
-            if n < 3:
-                prefix[h, n, :, :128], prefix[h, n, :, 128:] = m, v
-            else:
-                own[h, 0], own[h, 1] = m.astype(BF), v.astype(BF)
-            pairs[h] = m, v
+    ], {5: lambda: pass_on(1)})
+
+    def compose(n, m, v, h):
+        step = mm3(chain[n, h, 0], cat([m, v], 1))
+        return step[:, :128], step[:, 128:] + chain[n, h, 1]
+
+    low = [compose(1, chain[0, h, 0], chain[0, h, 1], h) for h in (0, 1)]
+    high = [compose(3, chain[2, h, 0], chain[2, h, 1], h) for h in (0, 1)]
+    for h in (0, 1):
+        step = mm3(high[h][0], cat(low[h], 1))
+        own[h, 0] = step[:, :128].astype(BF)
+        own[h, 1] = (step[:, 128:] + high[h][1]).astype(BF)
     swap = remote(
         own.at[1 - core, pl.ds(0, 2)], heard.at[pl.ds(0, 2)], esend.at[0], erecv.at[0], sibling
     )
     swap.start()
-    for h, rows in enumerate(HEADS):
-        qe[h, 0:CHUNK] = reads[0][rows].astype(BF)
-        for n in (1, 2, 3):
-            qe[h, CHUNK * n : CHUNK * n + CHUNK] = mm(
-                reads[n][rows], prefix[h, n - 1, :, :128]
-            ).astype(BF)
+    project(0, wcat, slice(0, 256), slice(0, 256), (2,))
+    for half in (0, 1):
+        for copy in fars[1, half][2:]:
+            copy.wait_recv()
+    project(*second_rows, (1, 3))
     swap.wait_recv()
     first = core == 0
     m0, b0 = [jnp.where(first, own[core, n], heard[n]) for n in (0, 1)]
     m1, b1 = [jnp.where(first, heard[n], own[core, n]) for n in (0, 1)]
+    m0t, m1t = [m.astype(F32).T.astype(BF) for m in (m0, m1)]
     both = mm(m1, cat([m0, b0], 1))
     comm[z, 0] = both[:, :128].astype(BF)
     comm[z, 1] = (both[:, 128:] + b1.astype(F32)).astype(BF)
@@ -375,7 +443,20 @@
     for copy in spread:
         copy.start()
 
-    project(1, wot, slice(768, 1024))
+    reads = together([query_pass(c, stacked(raw, c, 0), sf, sb) for c in range(CHUNKS)])
+    for h, rows in enumerate(HEADS):
+        for n, pair in ((0, (chain[0, h, 0], chain[0, h, 1])), (1, low[h]),
+                        (2, compose(2, *low[h], h))):
+            prefix[h, n, :, :128], prefix[h, n, :, 128:] = pair
+        qe[h, 0:CHUNK] = reads[0][rows].astype(BF)
+        for n in (1, 2, 3):
+            qe[h, CHUNK * n : CHUNK * n + CHUNK] = mm(
+                reads[n][rows], prefix[h, n - 1, :, :128]
+            ).astype(BF)
+    for half in (0, 1):
+        for copy in relays[1, half]:
+            copy.wait_recv()
+    project(*second_rows, (2,))
 
     for h in (0, 1):
         dO = raw[:, 768 + 128 * h : 896 + 128 * h]
@@ -386,7 +467,7 @@
     swap_l.wait_recv()
     l0 = jnp.where(first, own[core, 2], heard[2])
     l1 = jnp.where(first, heard[2], own[core, 2])
-    comm[z, 2] = (l0.astype(F32) + mm(m0, l1, 0, 0)).astype(BF)
+    comm[z, 2] = (l0.astype(F32) + mm(m0t, l1)).astype(BF)
     spread_l = [
         remote(comm.at[z, 2], comm.at[z, 2], esend.at[6 + o], erecv.at[6 + o], zs[o])
         for o in (1, 0, 2)
@@ -406,6 +487,20 @@
     give_s.start()
     states[core] = jnp.where(first, entering, after).astype(BF)
 
+    turned = [comm[n, 0].astype(F32).T.astype(BF) for n in range(3)]
+    across = mm(turned[1], turned[2])
+    eye = (iotas()[0] == iotas()[1]).astype(F32)
+    none = jnp.zeros_like(eye)
+    pull = cat([
+        jnp.where(z == 0, eye, none),
+        jnp.where(z == 1, eye, jnp.where(z == 0, turned[1].astype(F32), none)),
+        jnp.where(
+            z == 2, eye,
+            jnp.where(z == 1, turned[2].astype(F32), jnp.where(z == 0, across, none)),
+        ),
+    ], 1).astype(BF)
+    pull = cat([pull, mm(m1t, pull).astype(BF)])
+
     local = [[None] * CHUNKS, [None] * CHUNKS]
     turn = [[None] * CHUNKS, [None] * CHUNKS]
     for n in (3, 2, 1):
@@ -418,20 +513,25 @@
                 local[h][n - 1] = mm3(m, local[h][n], 0, 0) + step
                 turn[h][n - 1] = mm3(m, turn[h][n], 0, 0)
 
+    y0, pulls = [], []
+    for c in range(CHUNKS):
+        base = mm(sb[c, PT], stacked(raw, c, 768), 0, 0)
+        tk = sb[c, TK]
+        if c < 3:
+            base = base + cat([mm(tk[s], local[h][c]) for h, s in enumerate(HEADS)])
+            tk = cat([mm(tk[s], turn[h][c]) for h, s in enumerate(HEADS)]).astype(BF)
+        y0.append(base)
+        pulls.append(tk)
+
     for copy in spread_l:
         copy.wait_recv()
-    grad = comm[3, 2].astype(F32)
-    leaving = jnp.where(z == 2, grad, 0.0)
-    for n in (2, 1, 0):
-        grad = mm(comm[n, 0], grad, 0, 0) + comm[n, 2].astype(F32)
-        leaving = jnp.where(z == n - 1, grad, leaving)
-    before = mm(m1, leaving, 0, 0) + l1.astype(F32)
-    grads[2, 0] = jnp.where(first, leaving, before).astype(BF)
-    grads[2, 1] = grad.astype(BF)
+    last = comm[1:, 2].reshape(384, 128)
+    pulled = mm(pull, last)
+    leaving, before = pulled[:128], pulled[128:] + l1.astype(F32)
+    grads[2] = jnp.where(first, leaving, before).astype(BF)
     give_d = remote(grads.at[2], grads.at[core], esend.at[9], erecv.at[9], sibling)
     give_d.start()
-    grads[core, 0] = jnp.where(first, before, leaving).astype(BF)
-    grads[core, 1] = grad.astype(BF)
+    grads[core] = jnp.where(first, before, leaving).astype(BF)
     give_s.wait_recv()
     S = []
     for h in (0, 1):
@@ -452,37 +552,63 @@
         keep_rows(c, 0, dqr)
     give_d.wait_recv()
 
-    D = []
+    D, ends = [], [grads[0], grads[1]]
     for h in (0, 1):
-        sg_ref[h] = grads[h, 1].astype(F32)
-        d = grads[h, 0]
+        d = ends[h]
         D.append([mm(turn[h][n], d) + local[h][n] for n in range(3)] + [d])
 
-    def share(half, target):
+    def share(half, target, n):
         rows = gcat[128 * half : 128 * half + 128, :]
         if half == 0:
-            return mm(wcat[pl.ds(pl.multiple_of(576 * target, 16), 576), :], rows, 1, 1)
+            first_row = 576 * target + 288 * n
+            return mm(wcat[pl.ds(pl.multiple_of(first_row, 16), 288), :], rows, 1, 1)
         return cat([
-            mm(wcat[pl.ds(pl.multiple_of(576 * n + 144 * target, 16), 144), :], rows, 1, 1)
-            for n in range(4)
+            mm(wcat[pl.ds(pl.multiple_of(576 * k + 144 * target, 16), 144), :], rows, 1, 1)
+            for k in (2 * n, 2 * n + 1)
         ])
 
     outs = together([
-        third_pass(c, kept[c], [D[0][c], D[1][c]], sf, sb) for c in range(CHUNKS)
+        third_pass(c, kept[c], y0[c], pulls[c], ends, [D[0][c], D[1][c]], sf, sb) for c in range(CHUNKS)
     ])
     for c, (dkr, dv, _) in enumerate(outs):
         keep_rows(c, 256, dkr)
         keep_rows(c, 512, dv)
+    inner = (
+        last[:128].astype(F32) + mm(turned[1], last[128:256]) + mm(across, last[256:])
+    )
+    back = comm[0, 2].astype(F32) + mm(turned[0], inner)
+    origin[2] = back.astype(BF)
+    give_o = remote(origin.at[2], origin.at[core], esend.at[10], erecv.at[10], sibling)
+    give_o.start()
+    origin[core] = back.astype(BF)
+
+    lines = ((0, y, ys), (1, x, xs))
+
+    def send(half, slot, value, axis, forward):
+        part[half, slot] = value.astype(BF)
+        copy = remote(
+            part.at[half, slot], r1.at[half, slot], rsend.at[half, slot], rrecv.at[half, slot],
+            axis[forward],
+        )
+        copy.start()
+        return copy
+
     sums = [[], []]
-    for o in (1, 0, 2):
-        for half, place, axis in ((0, y, ys), (1, x, xs)):
-            part[half, o] = share(half, (place + o + 1) % 4).astype(BF)
-            copy = remote(
-                part.at[half, o], r1.at[half, o], rsend.at[half, 0, o], rrecv.at[half, 0, o],
-                axis[o],
+    for n, forward in ((0, 0), (1, 2)):
+        for half, place, axis in lines:
+            sums[half].append(
+                send(half, n, share(half, (place + 2) % 4, n), axis, forward)
             )
-            copy.start()
-            sums[half].append(copy)
+    for n, forward in ((1, 0), (0, 2)):
+        for half, place, axis in lines:
+            target = (place + forward + 1) % 4
+            sums[half].append(send(half, 3 - n, share(half, target, n), axis, forward))
+    for n, forward in ((0, 0), (1, 2)):
+        for half, place, axis in lines:
+            value = share(half, (place + forward + 1) % 4, n)
+            sums[half][n].wait_recv()
+            value = value + r1[half, n].astype(F32)
+            sums[half].append(send(half, 4 + n, value, axis, forward))
     for c, (dg, dbeta) in enumerate(together([
         last_pass(c, outs[c][2], sf, sb, passed) for c in range(CHUNKS)
     ])):
@@ -492,31 +618,33 @@
             bg_ref[h : h + 1, t] = jnp.sum(
                 jnp.where(diagonal, dbeta[s], 0.0), axis=0, keepdims=True
             )
-    ends = [[], []]
-    totals = [share(0, y), share(1, x)]
+    finals = [[], []]
+    totals = [cat([share(half, place, n) for n in (0, 1)]) for half, place, _ in lines]
     for half, place, axis in ((0, x, xs), (1, y, ys)):
-        total = totals[half]
-        for copy in sums[half]:
+        for copy in sums[half][2:]:
             copy.wait_recv()
-        for o in range(3):
-            total = total + r1[half, o].astype(F32)
+        got = [r1[half, n].astype(F32) for n in range(2, 6)]
+        total = totals[half] + cat([got[1] + got[2], got[0] + got[3]])
         t2f[half] = total.reshape(4, 144, 128)
         t2[half] = total.astype(BF).reshape(4, 144, 128)
         for o in (1, 0, 2):
             copy = remote(
                 t2.at[half, (place + o + 1) % 4], r2.at[half, o],
-                rsend.at[half, 1, o], rrecv.at[half, 1, o], axis[o],
+                rsend.at[half, 6 + o], rrecv.at[half, 6 + o], axis[o],
             )
             copy.start()
-            ends[half].append(copy)
+            finals[half].append(copy)
     done = []
     for half, place in ((0, x), (1, y)):
         total = t2f[half, place]
-        for copy in ends[half]:
+        for copy in finals[half]:
             copy.wait_recv()
         for o in range(3):
             total = total + r2[half, o].astype(F32)
         done.append(total)
+    give_o.wait_recv()
+    for h in (0, 1):
+        sg_ref[h] = origin[h].astype(F32)
     ig_ref[...] = cat(done, 1).astype(BF)
 
     for copy in sent:
@@ -556,7 +684,7 @@
             scratch(256, 1024),
             scratch(256, 768, dtype=BF),
             scratch(CHUNKS, 10, 128, 128),
-            scratch(CHUNKS, 9, 128, 128, dtype=BF),
+            scratch(CHUNKS, 10, 128, 128, dtype=BF),
             scratch(CHUNKS, 2, 2, 128, 128),
             scratch(CHUNKS, 8, 128),
             scratch(2, 3, 128, 256),
@@ -565,13 +693,14 @@
             scratch(3, 128, 128, dtype=BF),
             scratch(4, 3, 128, 128, dtype=BF),
             scratch(3, 128, 128, dtype=BF),
-            scratch(3, 2, 128, 128, dtype=BF),
-            scratch(2, 3, 576, 128, dtype=BF),
-            scratch(2, 3, 576, 128, dtype=BF),
+            scratch(3, 128, 128, dtype=BF),
+            scratch(3, 128, 128, dtype=BF),
+            scratch(2, 6, 288, 128, dtype=BF),
+            scratch(2, 6, 288, 128, dtype=BF),
             scratch(2, 4, 144, 128, dtype=BF),
             scratch(2, 4, 144, 128),
             scratch(2, 3, 144, 128, dtype=BF),
-            dma(4, 5), dma(2, 2, 2, 3), dma(2, 2, 2, 3), dma(10), dma(10), dma(2, 2, 3), dma(2, 2, 3),
+            dma(4, 5), dma(2, 2, 9), dma(2, 2, 9), dma(11), dma(11), dma(2, 9), dma(2, 9),
         ],
         compiler_params=pltpu.CompilerParams(
             collective_id=0, has_side_effects=True, vmem_limit_bytes=60 * 1024 * 1024

time: 55 us -> 51.9 us (0.944); the launches traced: 54 us -> 51.7 us
  Pallas kernels: 53.4 us -> 51.1 us
    pallas_call x1, Pallas kernels: 51.6 us -> 49.3 us  [per_device(): pl.pallas_call(kernel, out_shape=shapes, in_specs=[anywhere] * 10, out_sp...]
where the time goes in v4:
time: 51.9 us; the launch traced here: 51.7 us
  Pallas kernels  51.1 us (98%)
  between operations  0.64 us (1%)
    pallas_call x1, Pallas kernels, per_device(): pl.pallas_call(kernel, out_shape=shapes, in_specs=[anywhere] * 10, out_sp...  49.3 us
    pallas_call x1, Pallas kernels, per_device(): pl.pallas_call(finish, out_shape=shapes, in_specs=[vmem] * 4, out_specs=(...  1.81 us

profile of v4, /device:TPU:0, one launch (start us, length us, event | category | flops | bytes accessed | tf_op | source)
XLA Modules:
  0.0 51.7 jit_solution(5774089123444771862)
XLA Ops:
  0.6 49.3 %shard_map.129 = (bf16[144,256]{1,0:T(8,128)(2,1)}, f32[256,256]{1,0:T(8,128)}, f32[2,256]{1,0:T(2,128)}, f32[2,128,128]{2,1,0:T(8,128)}) custom-call(bf16[144,256]{1,0:T(8,128)(2,1)} %bitcast.3, bf16[144,256]{1,0:T(8,128)(2,1)} %bitcast.4, bf16[2304,256]{1,0:T(8,128)(2,1)} %wq_ref.1, bf16[2304,256]{1,0:T(8,128)(2,1)} %wk_ref.1, bf16[2304,256]{1,0:T(8,128)(2,1)} %wv_ref.1, ...), custom_call_target="tpu_custom_call" | custom-call | flops 3000000000 | bytes 6000000 | tf_op jit(solution)/shard_map/pallas_call | solution.py:670
  49.9 1.8 %shard_map.130 = (bf16[144,256]{1,0:T(8,128)(2,1)}, f32[256,256]{1,0:T(8,128)}, f32[2,256]{1,0:T(2,128)}, f32[2,128,128]{2,1,0:T(8,128)}) custom-call(bf16[144,256]{1,0:T(8,128)(2,1)} %get-tuple-element.12.refs_0_, f32[256,256]{1,0:T(8,128)} %get-tuple-element.13.refs_1_, f32[2,256]{1,0:T(2,128)} %get-tuple-element.14.refs_2_, ...), custom_call_target="tpu_custom_call" | custom-call | tf_op jit(solution)/shard_map/pallas_call | solution.py:712

commit v5 on v4

--- a/solution.py
+++ b/solution.py
@@ -234,7 +234,7 @@
 def kernel(
     x_ref, og_ref, wq_ref, wk_ref, wv_ref, wo_ref, gate_ref, beta_ref, init_ref, ds_ref,
     ig_ref, gg_ref, bg_ref, sg_ref,
-    gate, beta_in, start, ds, wcat, wo, wot, xg, raw, gcat, sf, sb, chain, passed, prefix, qe,
+    gg, bg, gate, beta_in, start, ds, wcat, wo, wot, xg, raw, gcat, sf, sb, chain, passed, prefix, qe,
     own, heard, comm, states, grads, origin, part, r1, t2, t2f, r2,
     wsem, gsend, grecv, esend, erecv, rsend, rrecv,
 ):
@@ -263,19 +263,17 @@
             (wo_ref, wo), (gate_ref, gate), (beta_ref, beta_in), (init_ref, start), (ds_ref, ds)
         ))
     ]
-    for load in loads:
-        load.start()
-
+    comm[...] = jnp.zeros_like(comm)
     barrier = pltpu.get_barrier_semaphore()
     partners = xs + ys + zs + [sibling]
     for device in partners:
         pl.semaphore_signal(barrier, inc=1, device_id=device, device_id_type=MESH)
 
+    for load in loads:
+        load.start()
     pl.semaphore_wait(barrier, len(partners))
 
     sent = []
-    for load in loads[:4]:
-        load.wait()
 
     def remote(src, dst, ssem, rsem, device):
         copy = pltpu.make_async_remote_copy(
@@ -287,21 +285,26 @@
 
     def near(item, half):
         block = xg.at[item, half, y, x]
+        source = (x_ref, og_ref)[item].at[:, 128 * half : 128 * half + 128]
         axis = xs if half == 0 else ys
         return [
-            remote(block, block, gsend.at[item, half, o], grecv.at[item, half, o], axis[o])
+            remote(source, block, gsend.at[item, half, o], grecv.at[item, half, o], axis[o])
             for o in (1, 0, 2)
         ]
 
-    def piece(item, half, group, n):
-        pair = pl.ds(2 * n, 2)
-        return xg.at[item, 0, group, pair] if half == 0 else xg.at[item, 1, pair, group]
+    def piece(item, half, group, first, count):
+        taken = pl.ds(first, count)
+        return xg.at[item, 0, group, taken] if half == 0 else xg.at[item, 1, taken, group]
 
     def far(item, half):
         place, axis = (y, ys) if half == 0 else (x, xs)
+        single = ((0, 0, 1), (2, 2, 1), (0, 1, 1), (2, 3, 1))
+        double = ((0, 0, 2), (2, 2, 2))
         copies = []
-        for n, (forward, number) in enumerate(((0, 0), (2, 1), (0, 1), (2, 0))):
-            block = piece(item, half, place, number)
+        for n, (forward, first, count) in enumerate(
+            (single if item == 0 else double) + ((0, 2, 2), (2, 0, 2))
+        ):
+            block = piece(item, half, place, first, count)
             copies.append(remote(
                 block, block, gsend.at[item, half, 3 + n], grecv.at[item, half, 3 + n],
                 axis[forward],
@@ -310,11 +313,14 @@
 
     def hand_on(item, half):
         place, axis = (y, ys) if half == 0 else (x, xs)
+        single = ((0, 0, 1), (2, 2, 1), (0, 1, 1), (2, 3, 1))
+        double = ((0, 0, 2), (2, 2, 2))
         copies = []
-        for n, (forward, group) in enumerate(((0, (place + 3) % 4), (2, (place + 1) % 4))):
-            block = piece(item, half, group, n)
+        for n, (forward, first, count) in enumerate(single if item == 0 else double):
+            group = (place + 3) % 4 if forward == 0 else (place + 1) % 4
+            block = piece(item, half, group, first, count)
             copies.append(remote(
-                block, block, gsend.at[item, half, 7 + n], grecv.at[item, half, 7 + n],
+                block, block, gsend.at[item, half, 9 + n], grecv.at[item, half, 9 + n],
                 axis[forward],
             ))
         return copies
@@ -333,12 +339,12 @@
         for half in (0, 1):
             for copy in nears[item, half]:
                 copy.wait_recv()
-        for n in range(4):
+        for n in range(len(fars[item, 0])):
             for half in (0, 1):
                 fars[item, half][n].start()
 
     def pass_on(item):
-        for n in (0, 1):
+        for n in range(len(relays[item, 0])):
             for half in (0, 1):
                 fars[item, half][n].wait_recv()
                 relays[item, half][n].start()
@@ -365,6 +371,8 @@
 
     begin(0)
     begin(1)
+    for load in loads[:4]:
+        load.wait()
     widen(0)
     for load in loads[4:]:
         load.wait()
@@ -376,7 +384,7 @@
     for n in range(18):
         wot[128 * n : 128 * n + 128, :] = wo[:, 128 * n : 128 * n + 128].T
     for half in (0, 1):
-        for copy in fars[0, half][2:]:
+        for copy in fars[0, half][4:]:
             copy.wait_recv()
     project(*first_rows, (1, 3))
     project(*second_rows, (0,))
@@ -406,7 +414,7 @@
             stacked(gate, c, 0), betas[c], ds, sf, sb, chain, passed,
         )
         for c in range(CHUNKS)
-    ], {5: lambda: pass_on(1)})
+    ], {2: lambda: pass_on(1)})
 
     def compose(n, m, v, h):
         step = mm3(chain[n, h, 0], cat([m, v], 1))
@@ -423,10 +431,7 @@
     )
     swap.start()
     project(0, wcat, slice(0, 256), slice(0, 256), (2,))
-    for half in (0, 1):
-        for copy in fars[1, half][2:]:
-            copy.wait_recv()
-    project(*second_rows, (1, 3))
+    reads = together([query_pass(c, stacked(raw, c, 0), sf, sb) for c in range(CHUNKS)])
     swap.wait_recv()
     first = core == 0
     m0, b0 = [jnp.where(first, own[core, n], heard[n]) for n in (0, 1)]
@@ -435,15 +440,24 @@
     both = mm(m1, cat([m0, b0], 1))
     comm[z, 0] = both[:, :128].astype(BF)
     comm[z, 1] = (both[:, 128:] + b1.astype(F32)).astype(BF)
-    spread = [
-        remote(comm.at[z, pl.ds(0, 2)], comm.at[z, pl.ds(0, 2)], esend.at[1 + o],
-               erecv.at[1 + o], zs[o])
-        for o in (1, 0, 2)
-    ]
-    for copy in spread:
-        copy.start()
-
-    reads = together([query_pass(c, stacked(raw, c, 0), sf, sb) for c in range(CHUNKS)])
+    def line(first, count, number, o):
+        block = comm.at[z, pl.ds(first, count)]
+        return pltpu.make_async_remote_copy(
+            src_ref=block, dst_ref=block, send_sem=esend.at[number], recv_sem=erecv.at[number],
+            device_id=zs[o - 1], device_id_type=MESH,
+        )
+
+    both_maps = {o: line(0, 2, o, o) for o in (1, 2, 3)}
+    one_map = {o: line(0, 1, o, o) for o in (1, 2, 3)}
+    back = {o: line(2, 1, 5 + o, o) for o in (1, 2, 3)}
+    for o in (2, 1, 3):
+        pl.when(z < 4 - o)(both_maps[o].start)
+        pl.when(z >= 4 - o)(one_map[o].start)
+
+    for half in (0, 1):
+        for copy in fars[1, half][2:]:
+            copy.wait_recv()
+    project(*second_rows, (1, 3))
     for h, rows in enumerate(HEADS):
         for n, pair in ((0, (chain[0, h, 0], chain[0, h, 1])), (1, low[h]),
                         (2, compose(2, *low[h], h))):
@@ -464,19 +478,17 @@
     swap_l = remote(own.at[1 - core, 2], heard.at[2], esend.at[4], erecv.at[4], sibling)
     swap_l.start()
 
+    bases = [mm(sb[c, PT], stacked(raw, c, 768), 0, 0) for c in range(CHUNKS)]
     swap_l.wait_recv()
     l0 = jnp.where(first, own[core, 2], heard[2])
     l1 = jnp.where(first, heard[2], own[core, 2])
     comm[z, 2] = (l0.astype(F32) + mm(m0t, l1)).astype(BF)
-    spread_l = [
-        remote(comm.at[z, 2], comm.at[z, 2], esend.at[6 + o], erecv.at[6 + o], zs[o])
-        for o in (1, 0, 2)
-    ]
-    for copy in spread_l:
-        copy.start()
-
-    for copy in spread:
-        copy.wait_recv()
+    for o in (2, 1, 3):
+        pl.when(z >= 4 - o)(back[o].start)
+
+    for o in (1, 2, 3):
+        pl.when(z >= o)(both_maps[o].wait_recv)
+        pl.when(z < o)(one_map[o].wait_recv)
     state, entering = start[core], start[core]
     for n in range(3):
         state = mm(comm[n, 0], state) + comm[n, 1].astype(F32)
@@ -515,7 +527,7 @@
 
     y0, pulls = [], []
     for c in range(CHUNKS):
-        base = mm(sb[c, PT], stacked(raw, c, 768), 0, 0)
+        base = bases[c]
         tk = sb[c, TK]
         if c < 3:
             base = base + cat([mm(tk[s], local[h][c]) for h, s in enumerate(HEADS)])
@@ -523,8 +535,8 @@
         y0.append(base)
         pulls.append(tk)
 
-    for copy in spread_l:
-        copy.wait_recv()
+    for o in (1, 2, 3):
+        pl.when(z < o)(back[o].wait_recv)
     last = comm[1:, 2].reshape(384, 128)
     pulled = mm(pull, last)
     leaving, before = pulled[:128], pulled[128:] + l1.astype(F32)
@@ -576,61 +588,87 @@
     inner = (
         last[:128].astype(F32) + mm(turned[1], last[128:256]) + mm(across, last[256:])
     )
-    back = comm[0, 2].astype(F32) + mm(turned[0], inner)
-    origin[2] = back.astype(BF)
-    give_o = remote(origin.at[2], origin.at[core], esend.at[10], erecv.at[10], sibling)
-    give_o.start()
-    origin[core] = back.astype(BF)
+    origin[2] = (comm[0, 2].astype(F32) + mm(turned[0], inner)).astype(BF)
+    tell = {
+        o: pltpu.make_async_remote_copy(
+            src_ref=origin.at[2], dst_ref=origin.at[3], send_sem=esend.at[10 + o],
+            recv_sem=erecv.at[10 + o], device_id=zs[o - 1], device_id_type=MESH,
+        )
+        for o in (1, 2, 3)
+    }
+    for o in (1, 2, 3):
+        pl.when(z == 0)(tell[o].start)
 
     lines = ((0, y, ys), (1, x, xs))
 
-    def send(half, slot, value, axis, forward):
-        part[half, slot] = value.astype(BF)
+    def send(half, slot, count, axis, forward):
+        block = part.at[half, pl.ds(slot, count)]
         copy = remote(
-            part.at[half, slot], r1.at[half, slot], rsend.at[half, slot], rrecv.at[half, slot],
+            block, r1.at[half, pl.ds(slot, count)], rsend.at[half, slot], rrecv.at[half, slot],
             axis[forward],
         )
         copy.start()
         return copy
 
-    sums = [[], []]
+    def keep(half, slot, value):
+        count = value.shape[0] // 144
+        part[half, slot : slot + count] = value.astype(BF).reshape(count, 144, 128)
+
+    sums = [[None] * 10, [None] * 10]
     for n, forward in ((0, 0), (1, 2)):
         for half, place, axis in lines:
-            sums[half].append(
-                send(half, n, share(half, (place + 2) % 4, n), axis, forward)
-            )
+            keep(half, 2 * n, share(half, (place + 2) % 4, n))
+            for slot in (2 * n, 2 * n + 1):
+                sums[half][slot] = send(half, slot, 1, axis, forward)
     for n, forward in ((1, 0), (0, 2)):
         for half, place, axis in lines:
-            target = (place + forward + 1) % 4
-            sums[half].append(send(half, 3 - n, share(half, target, n), axis, forward))
-    for n, forward in ((0, 0), (1, 2)):
-        for half, place, axis in lines:
-            value = share(half, (place + forward + 1) % 4, n)
-            sums[half][n].wait_recv()
-            value = value + r1[half, n].astype(F32)
-            sums[half].append(send(half, 4 + n, value, axis, forward))
+            keep(half, 4 + 2 * n, share(half, (place + forward + 1) % 4, n))
+            sums[half][4 + n] = send(half, 4 + 2 * n, 2, axis, forward)
+    added = {
+        (half, n): share(half, (place + forward + 1) % 4, n)
+        for n, forward in ((0, 0), (1, 2)) for half, place, _ in lines
+    }
+    for k in (0, 1):
+        for n, forward in ((0, 0), (1, 2)):
+            for half, place, axis in lines:
+                slot = 2 * n + k
+                sums[half][slot].wait_recv()
+                value = added[half, n][144 * k : 144 * k + 144] + r1[half, slot].astype(F32)
+                keep(half, 8 + slot, value)
+                sums[half][6 + slot] = send(half, 8 + slot, 1, axis, forward)
     for c, (dg, dbeta) in enumerate(together([
         last_pass(c, outs[c][2], sf, sb, passed) for c in range(CHUNKS)
     ])):
         t = slice(CHUNK * c, CHUNK * c + CHUNK)
         for h, s in enumerate(HEADS):
-            gg_ref[t, 128 * h : 128 * h + 128] = dg[s]
-            bg_ref[h : h + 1, t] = jnp.sum(
+            gg[t, 128 * h : 128 * h + 128] = dg[s]
+            bg[h : h + 1, t] = jnp.sum(
                 jnp.where(diagonal, dbeta[s], 0.0), axis=0, keepdims=True
             )
+    stores = [
+        pltpu.make_async_copy(gg, gg_ref, wsem.at[0, 2]),
+        pltpu.make_async_copy(bg, bg_ref, wsem.at[0, 3]),
+    ]
+    for store in stores:
+        store.start()
+    for o in (1, 2, 3):
+        pl.when(z == o)(tell[o].wait_recv)
+    origin[core] = jnp.where(z == 0, origin[2], origin[3])
+    give_o = remote(origin.at[core], origin.at[core], esend.at[10], erecv.at[10], sibling)
+    give_o.start()
     finals = [[], []]
     totals = [cat([share(half, place, n) for n in (0, 1)]) for half, place, _ in lines]
     for half, place, axis in ((0, x, xs), (1, y, ys)):
-        for copy in sums[half][2:]:
+        for copy in sums[half][4:]:
             copy.wait_recv()
-        got = [r1[half, n].astype(F32) for n in range(2, 6)]
-        total = totals[half] + cat([got[1] + got[2], got[0] + got[3]])
-        t2f[half] = total.reshape(4, 144, 128)
-        t2[half] = total.astype(BF).reshape(4, 144, 128)
+        got = [r1[half, 4 * n : 4 * n + 4].astype(F32) for n in (1, 2)]
+        total = totals[half].reshape(4, 144, 128) + got[0] + got[1]
+        t2f[half] = total
+        t2[half] = total.astype(BF)
         for o in (1, 0, 2):
             copy = remote(
                 t2.at[half, (place + o + 1) % 4], r2.at[half, o],
-                rsend.at[half, 6 + o], rrecv.at[half, 6 + o], axis[o],
+                rsend.at[half, 12 + o], rrecv.at[half, 12 + o], axis[o],
             )
             copy.start()
             finals[half].append(copy)
@@ -646,7 +684,14 @@
     for h in (0, 1):
         sg_ref[h] = origin[h].astype(F32)
     ig_ref[...] = cat(done, 1).astype(BF)
-
+    for store in stores:
+        store.wait()
+
+    for o in (1, 2, 3):
+        pl.when(z < 4 - o)(both_maps[o].wait_send)
+        pl.when(z >= 4 - o)(one_map[o].wait_send)
+        pl.when(z >= 4 - o)(back[o].wait_send)
+        pl.when(z == 0)(tell[o].wait_send)
     for copy in sent:
         copy.wait_send()
 
@@ -671,8 +716,10 @@
         kernel,
         out_shape=shapes,
         in_specs=[anywhere] * 10,
-        out_specs=(vmem,) * 4,
+        out_specs=(vmem, anywhere, anywhere, vmem),
         scratch_shapes=[
+            scratch(256, 256),
+            scratch(2, 256),
             scratch(256, 256),
             scratch(2, 256),
             scratch(2, 128, 128),
@@ -694,13 +741,13 @@
             scratch(4, 3, 128, 128, dtype=BF),
             scratch(3, 128, 128, dtype=BF),
             scratch(3, 128, 128, dtype=BF),
-            scratch(3, 128, 128, dtype=BF),
-            scratch(2, 6, 288, 128, dtype=BF),
-            scratch(2, 6, 288, 128, dtype=BF),
+            scratch(4, 128, 128, dtype=BF),
+            scratch(2, 12, 144, 128, dtype=BF),
+            scratch(2, 12, 144, 128, dtype=BF),
             scratch(2, 4, 144, 128, dtype=BF),
             scratch(2, 4, 144, 128),
             scratch(2, 3, 144, 128, dtype=BF),
-            dma(4, 5), dma(2, 2, 9), dma(2, 2, 9), dma(11), dma(11), dma(2, 9), dma(2, 9),
+            dma(4, 5), dma(2, 2, 13), dma(2, 2, 13), dma(14), dma(14), dma(2, 15), dma(2, 15),
         ],
         compiler_params=pltpu.CompilerParams(
             collective_id=0, has_side_effects=True, vmem_limit_bytes=60 * 1024 * 1024

time: 51.9 us -> 51 us (0.983)
  Pallas kernels: 51.1 us -> 50.2 us
    pallas_call x1, Pallas kernels: 49.3 us -> 48.4 us  [per_device(): pl.pallas_call(kernel, out_shape=shapes, in_specs=[anywhere] * 10, out_sp...]
where the time goes in v5:
time: 51 us; the launch traced here: 50.9 us
  Pallas kernels  50.2 us (98%)
  between operations  0.64 us (1%)
    pallas_call x1, Pallas kernels, per_device(): pl.pallas_call(kernel, out_shape=shapes, in_specs=[anywhere] * 10, out_sp...  48.4 us
    pallas_call x1, Pallas kernels, per_device(): pl.pallas_call(finish, out_shape=shapes, in_specs=[vmem] * 4, out_specs=(...  1.81 us

profile of v5, /device:TPU:0, one launch (start us, length us, event | category | flops | bytes accessed | tf_op | source)
XLA Modules:
  0.0 50.9 jit_solution(7657800376222797456)
XLA Ops:
  0.6 48.4 %shard_map.129 = (bf16[144,256]{1,0:T(8,128)(2,1)}, f32[256,256]{1,0:T(8,128)}, f32[2,256]{1,0:T(2,128)}, f32[2,128,128]{2,1,0:T(8,128)}) custom-call(bf16[144,256]{1,0:T(8,128)(2,1)} %bitcast.3, bf16[144,256]{1,0:T(8,128)(2,1)} %bitcast.4, bf16[2304,256]{1,0:T(8,128)(2,1)} %wq_ref.1, bf16[2304,256]{1,0:T(8,128)(2,1)} %wk_ref.1, bf16[2304,256]{1,0:T(8,128)(2,1)} %wv_ref.1, ...), custom_call_target="tpu_custom_call" | custom-call | flops 3000000000 | bytes 6000000 | tf_op jit(solution)/shard_map/pallas_call | solution.py:715
  49.1 1.8 %shard_map.130 = (bf16[144,256]{1,0:T(8,128)(2,1)}, f32[256,256]{1,0:T(8,128)}, f32[2,256]{1,0:T(2,128)}, f32[2,128,128]{2,1,0:T(8,128)}) custom-call(bf16[144,256]{1,0:T(8,128)(2,1)} %get-tuple-element.12.refs_0_, f32[256,256]{1,0:T(8,128)} %get-tuple-element.13.refs_1_, f32[2,256]{1,0:T(2,128)} %get-tuple-element.14.refs_2_, ...), custom_call_target="tpu_custom_call" | custom-call | tf_op jit(solution)/shard_map/pallas_call | solution.py:759

commit v6 on v5

--- a/solution.py
+++ b/solution.py
@@ -79,12 +79,14 @@
     yield
     t = mm(p, eye + d8)
     yield
-    for s in (4, 5):
-        off = jnp.where(((i >> (s + 1)) == (j >> (s + 1))) & ((i >> s) != (j >> s)), n, 0.0)
-        step = mm(off, t)
-        yield
-        t = t - mm(t, step)
-        yield
+    off = jnp.where(((i >> 6) == (j >> 6)) & ((i >> 4) != (j >> 4)), n, 0.0)
+    e = mm(t, off)
+    yield
+    e2 = mm(e, e)
+    r = t - mm(e, t)
+    yield
+    t = r + mm(e2, r)
+    yield
     return t
 
 
@@ -298,12 +300,11 @@
 
     def far(item, half):
         place, axis = (y, ys) if half == 0 else (x, xs)
-        single = ((0, 0, 1), (2, 2, 1), (0, 1, 1), (2, 3, 1))
-        double = ((0, 0, 2), (2, 2, 2))
+        pieces = ((0, 0, 1), (2, 2, 1), (0, 1, 1), (2, 3, 1), (0, 2, 2), (2, 0, 2))
+        if item == 1:
+            pieces = ((0, 0, 4), (2, 0, 4), (1, 0, 4))
         copies = []
-        for n, (forward, first, count) in enumerate(
-            (single if item == 0 else double) + ((0, 2, 2), (2, 0, 2))
-        ):
+        for n, (forward, first, count) in enumerate(pieces):
             block = piece(item, half, place, first, count)
             copies.append(remote(
                 block, block, gsend.at[item, half, 3 + n], grecv.at[item, half, 3 + n],
@@ -313,10 +314,9 @@
 
     def hand_on(item, half):
         place, axis = (y, ys) if half == 0 else (x, xs)
-        single = ((0, 0, 1), (2, 2, 1), (0, 1, 1), (2, 3, 1))
-        double = ((0, 0, 2), (2, 2, 2))
+        pieces = ((0, 0, 1), (2, 2, 1), (0, 1, 1), (2, 3, 1))
         copies = []
-        for n, (forward, first, count) in enumerate(single if item == 0 else double):
+        for n, (forward, first, count) in enumerate(pieces):
             group = (place + 3) % 4 if forward == 0 else (place + 1) % 4
             block = piece(item, half, group, first, count)
             copies.append(remote(
@@ -328,7 +328,7 @@
     parts = [(item, half) for item in (0, 1) for half in (0, 1)]
     nears = {part: near(*part) for part in parts}
     fars = {part: far(*part) for part in parts}
-    relays = {part: hand_on(*part) for part in parts}
+    relays = {part: hand_on(*part) for part in parts[:2]}
 
     def begin(item):
         for o in range(3):
@@ -414,7 +414,7 @@
             stacked(gate, c, 0), betas[c], ds, sf, sb, chain, passed,
         )
         for c in range(CHUNKS)
-    ], {2: lambda: pass_on(1)})
+    ])
 
     def compose(n, m, v, h):
         step = mm3(chain[n, h, 0], cat([m, v], 1))
@@ -422,6 +422,7 @@
 
     low = [compose(1, chain[0, h, 0], chain[0, h, 1], h) for h in (0, 1)]
     high = [compose(3, chain[2, h, 0], chain[2, h, 1], h) for h in (0, 1)]
+    third = [compose(2, *low[h], h) for h in (0, 1)]
     for h in (0, 1):
         step = mm3(high[h][0], cat(low[h], 1))
         own[h, 0] = step[:, :128].astype(BF)
@@ -432,6 +433,19 @@
     swap.start()
     project(0, wcat, slice(0, 256), slice(0, 256), (2,))
     reads = together([query_pass(c, stacked(raw, c, 0), sf, sb) for c in range(CHUNKS)])
+    for h, rows in enumerate(HEADS):
+        for n, pair in ((0, (chain[0, h, 0], chain[0, h, 1])), (1, low[h]),
+                        (2, third[h])):
+            prefix[h, n, :, :128], prefix[h, n, :, 128:] = pair
+        qe[h, 0:CHUNK] = reads[0][rows].astype(BF)
+        for n in (1, 2, 3):
+            qe[h, CHUNK * n : CHUNK * n + CHUNK] = mm(
+                reads[n][rows], prefix[h, n - 1, :, :128]
+            ).astype(BF)
+    for half in (0, 1):
+        for copy in fars[1, half][:2]:
+            copy.wait_recv()
+    project(*second_rows, (1, 3))
     swap.wait_recv()
     first = core == 0
     m0, b0 = [jnp.where(first, own[core, n], heard[n]) for n in (0, 1)]
@@ -455,21 +469,7 @@
         pl.when(z >= 4 - o)(one_map[o].start)
 
     for half in (0, 1):
-        for copy in fars[1, half][2:]:
-            copy.wait_recv()
-    project(*second_rows, (1, 3))
-    for h, rows in enumerate(HEADS):
-        for n, pair in ((0, (chain[0, h, 0], chain[0, h, 1])), (1, low[h]),
-                        (2, compose(2, *low[h], h))):
-            prefix[h, n, :, :128], prefix[h, n, :, 128:] = pair
-        qe[h, 0:CHUNK] = reads[0][rows].astype(BF)
-        for n in (1, 2, 3):
-            qe[h, CHUNK * n : CHUNK * n + CHUNK] = mm(
-                reads[n][rows], prefix[h, n - 1, :, :128]
-            ).astype(BF)
-    for half in (0, 1):
-        for copy in relays[1, half]:
-            copy.wait_recv()
+        fars[1, half][2].wait_recv()
     project(*second_rows, (2,))
 
     for h in (0, 1):
@@ -513,25 +513,25 @@
     ], 1).astype(BF)
     pull = cat([pull, mm(m1t, pull).astype(BF)])
 
-    local = [[None] * CHUNKS, [None] * CHUNKS]
-    turn = [[None] * CHUNKS, [None] * CHUNKS]
+    suffix = [[None] * 3, [None] * 3]
     for n in (3, 2, 1):
         for h, rows in enumerate(HEADS):
             step = mm(reads[n][rows], stacked(raw, n, 768)[rows], 0, 0)
-            m = chain[n, h, 0]
+            m = chain[n, h, 0].T
             if n == 3:
-                local[h][2], turn[h][2] = step, m.T
+                suffix[h][2] = cat([m, step], 1)
             else:
-                local[h][n - 1] = mm3(m, local[h][n], 0, 0) + step
-                turn[h][n - 1] = mm3(m, turn[h][n], 0, 0)
+                value = mm(m, suffix[h][n])
+                suffix[h][n - 1] = cat([value[:, :128], value[:, 128:] + step], 1)
 
     y0, pulls = [], []
     for c in range(CHUNKS):
         base = bases[c]
         tk = sb[c, TK]
         if c < 3:
-            base = base + cat([mm(tk[s], local[h][c]) for h, s in enumerate(HEADS)])
-            tk = cat([mm(tk[s], turn[h][c]) for h, s in enumerate(HEADS)]).astype(BF)
+            value = cat([mm(tk[s], suffix[h][c]) for h, s in enumerate(HEADS)])
+            base = base + value[:, 128:]
+            tk = value[:, :128].astype(BF)
         y0.append(base)
         pulls.append(tk)
 
@@ -548,7 +548,8 @@
     S = []
     for h in (0, 1):
         s = states[h]
-        S.append([s] + [mm(prefix[h, n, :, :128], s) + prefix[h, n, :, 128:] for n in range(3)])
+        value = mm(prefix[h, :, :, :128].reshape(384, 128), s).reshape(3, 128, 128)
+        S.append([s] + [value[n] + prefix[h, n, :, 128:] for n in range(3)])
     outs = together([
         second_pass(c, [S[0][c], S[1][c]], stacked(raw, c, 768), sf, sb) for c in range(CHUNKS)
     ])
@@ -567,7 +568,8 @@
     D, ends = [], [grads[0], grads[1]]
     for h in (0, 1):
         d = ends[h]
-        D.append([mm(turn[h][n], d) + local[h][n] for n in range(3)] + [d])
+        value = mm(cat([suffix[h][n][:, :128] for n in range(3)]), d).reshape(3, 128, 128)
+        D.append([value[n] + suffix[h][n][:, 128:] for n in range(3)] + [d])
 
     def share(half, target, n):
         rows = gcat[128 * half : 128 * half + 128, :]

time: 51 us -> 50.5 us (level)
    pallas_call x1, Pallas kernels: 48.4 us -> 47.9 us  [per_device(): pl.pallas_call(kernel, out_shape=shapes, in_specs=[anywhere] * 10, out_sp...]
where the time goes in v6:
time: 50.5 us; the launch traced here: 50.4 us
  Pallas kernels  49.7 us (98%)
  between operations  0.64 us (1%)
    pallas_call x1, Pallas kernels, per_device(): pl.pallas_call(kernel, out_shape=shapes, in_specs=[anywhere] * 10, out_sp...  47.9 us
    pallas_call x1, Pallas kernels, per_device(): pl.pallas_call(finish, out_shape=shapes, in_specs=[vmem] * 4, out_specs=(...  1.81 us

profile of v6, /device:TPU:0, one launch (start us, length us, event | category | flops | bytes accessed | tf_op | source)
XLA Modules:
  0.0 50.4 jit_solution(17160068515051118452)
XLA Ops:
  0.6 47.9 %shard_map.129 = (bf16[144,256]{1,0:T(8,128)(2,1)}, f32[256,256]{1,0:T(8,128)}, f32[2,256]{1,0:T(2,128)}, f32[2,128,128]{2,1,0:T(8,128)}) custom-call(bf16[144,256]{1,0:T(8,128)(2,1)} %bitcast.3, bf16[144,256]{1,0:T(8,128)(2,1)} %bitcast.4, bf16[2304,256]{1,0:T(8,128)(2,1)} %wq_ref.1, bf16[2304,256]{1,0:T(8,128)(2,1)} %wk_ref.1, bf16[2304,256]{1,0:T(8,128)(2,1)} %wv_ref.1, ...), custom_call_target="tpu_custom_call" | custom-call | flops 3000000000 | bytes 6000000 | tf_op jit(solution)/shard_map/pallas_call | solution.py:717
  48.5 1.8 %shard_map.130 = (bf16[144,256]{1,0:T(8,128)(2,1)}, f32[256,256]{1,0:T(8,128)}, f32[2,256]{1,0:T(2,128)}, f32[2,128,128]{2,1,0:T(8,128)}) custom-call(bf16[144,256]{1,0:T(8,128)(2,1)} %get-tuple-element.12.refs_0_, f32[256,256]{1,0:T(8,128)} %get-tuple-element.13.refs_1_, f32[2,256]{1,0:T(2,128)} %get-tuple-element.14.refs_2_, ...), custom_call_target="tpu_custom_call" | custom-call | tf_op jit(solution)/shard_map/pallas_call | solution.py:761

commit v7 on v6

--- a/solution.py
+++ b/solution.py
@@ -265,7 +265,7 @@
             (wo_ref, wo), (gate_ref, gate), (beta_ref, beta_in), (init_ref, start), (ds_ref, ds)
         ))
     ]
-    comm[...] = jnp.zeros_like(comm)
+    comm[1:, 2] = jnp.zeros((3, 128, 128), BF)
     barrier = pltpu.get_barrier_semaphore()
     partners = xs + ys + zs + [sibling]
     for device in partners:

time: 50.5 us -> 50.5 us (level)
  no operation moved by 1% of the time
where the time goes in v7:
time: 50.5 us; the launch traced here: 50.4 us
  Pallas kernels  49.7 us (98%)
  between operations  0.64 us (1%)
    pallas_call x1, Pallas kernels, per_device(): pl.pallas_call(kernel, out_shape=shapes, in_specs=[anywhere] * 10, out_sp...  47.9 us
    pallas_call x1, Pallas kernels, per_device(): pl.pallas_call(finish, out_shape=shapes, in_specs=[vmem] * 4, out_specs=(...  1.81 us

profile of v7, /device:TPU:0, one launch (start us, length us, event | category | flops | bytes accessed | tf_op | source)
XLA Modules:
  0.0 50.4 jit_solution(9155831486858664099)
XLA Ops:
  0.6 47.9 %shard_map.129 = (bf16[144,256]{1,0:T(8,128)(2,1)}, f32[256,256]{1,0:T(8,128)}, f32[2,256]{1,0:T(2,128)}, f32[2,128,128]{2,1,0:T(8,128)}) custom-call(bf16[144,256]{1,0:T(8,128)(2,1)} %bitcast.3, bf16[144,256]{1,0:T(8,128)(2,1)} %bitcast.4, bf16[2304,256]{1,0:T(8,128)(2,1)} %wq_ref.1, bf16[2304,256]{1,0:T(8,128)(2,1)} %wk_ref.1, bf16[2304,256]{1,0:T(8,128)(2,1)} %wv_ref.1, ...), custom_call_target="tpu_custom_call" | custom-call | flops 3000000000 | bytes 6000000 | tf_op jit(solution)/shard_map/pallas_call | solution.py:717
  48.5 1.8 %shard_map.130 = (bf16[144,256]{1,0:T(8,128)(2,1)}, f32[256,256]{1,0:T(8,128)}, f32[2,256]{1,0:T(2,128)}, f32[2,128,128]{2,1,0:T(8,128)}) custom-call(bf16[144,256]{1,0:T(8,128)(2,1)} %get-tuple-element.12.refs_0_, f32[256,256]{1,0:T(8,128)} %get-tuple-element.13.refs_1_, f32[2,256]{1,0:T(2,128)} %get-tuple-element.14.refs_2_, ...), custom_call_target="tpu_custom_call" | custom-call | tf_op jit(solution)/shard_map/pallas_call | solution.py:761
